TPU v7x, 512 devices: a whole 4x4x16 slice. The times are simulated.
512 devices in a mesh: depth: 8 (over x_lo, y), azim: 64 (over z, x_hi, core).
Axes of the slice: x: 4 (x_hi: 2, x_lo: 2; x = x_hi * 2 + x_lo), y: 4, z: 16, core: 2. Of those that a mesh axis runs over, the one named last changes fastest.
Arguments:
- cotangent: bfloat16 [128, 4096, 256], P('depth', 'azim'), may hold values from -6 to 6
- pre_second: bfloat16 [128, 4096, 256], P('depth', 'azim'), may hold values from -6 to 6
- pre_first: bfloat16 [128, 4096, 256], P('depth', 'azim'), may hold values from -6 to 6
- kernel_first: bfloat16 [3, 3, 3, 32, 32], replicated, may hold values from -0.21875 to 0.21875
- kernel_second: bfloat16 [3, 3, 3, 32, 32], replicated, may hold values from -0.21875 to 0.21875
- row_resample: float32 [4, 128, 8, 8], P(None, 'depth'), may hold values from -0.1875 to 0.1875
- col_taps: float32 [4, 128, 8], P(None, 'depth'), may hold values from 0.1 to 1
- band_width: int32 [4, 128], P(None, 'depth'), may hold values from 1 to 8
- col_offset: int32 [4, 128], P(None, 'depth'), may hold values from -24 to 24, as said below
Outputs:
- cam_grad: float32 [8, 4096, 128], P('depth', 'azim')
Inputs may be any that keep to these rules, and one draw needn't show every extreme that they name: `col_offset`: some entry equals -24 and some entry equals 24.
All inputs are finite; a program needn't handle non-finite values.
Results may differ from a plain program's by a relative error of at most 0.0048.
Values may be sent and summed in bfloat16 or wider, within the bound.
A program may use at most 64 MiB of HBM per device.

v0:
```python
import jax
import jax.numpy as jnp
from jax import lax
from jax.sharding import PartitionSpec as P

TAPS = 8
SHIFT = 24


def padded_2(block, sides, width):
    for axis, dim in sides:
        count = lax.axis_size(axis)
        forward = [(i, i + 1) for i in range(count - 1)]
        forward.append((count - 1, 0))
        backward = [(target, source) for source, target in forward]
        low = lax.ppermute(
            lax.slice_in_dim(block, block.shape[dim] - width, None, axis=dim), axis, forward
        )
        high = lax.ppermute(lax.slice_in_dim(block, 0, width, axis=dim), axis, backward)
        block = jnp.concatenate([low, block, high], axis=dim)
    return block


def row_mixers(kernel, row_count):
    channels = kernel.shape[3]
    row_in = lax.broadcasted_iota(jnp.int32, (row_count, 1, row_count, 1), 0)
    row_out = lax.broadcasted_iota(jnp.int32, (row_count, 1, row_count, 1), 2)
    mixers = []
    for depth_tap in range(3):
        group = []
        for column_tap in range(3):
            mixed = jnp.zeros((row_count, channels, row_count, channels), jnp.bfloat16)
            for row_tap in range(3):
                block = kernel[depth_tap, column_tap, row_tap].T[None, :, None, :]
                mixed = mixed + jnp.where(
                    row_in == row_out + 1 - row_tap, block, jnp.zeros((), jnp.bfloat16)
                )
            group.append(mixed.reshape(row_count * channels, row_count * channels))
        mixers.append(group)
    return mixers


def transpose_conv(padded, mixers):
    sphere_span, column_span, merged = padded.shape
    out_spheres = sphere_span - 2
    out_columns = column_span - 2
    accumulated = jnp.zeros((out_spheres * out_columns, merged), jnp.float32)
    for depth_tap in range(3):
        for column_tap in range(3):
            slab = padded[
                2 - depth_tap : 2 - depth_tap + out_spheres,
                2 - column_tap : 2 - column_tap + out_columns,
            ]
            accumulated = accumulated + jnp.dot(
                slab.reshape(-1, merged),
                mixers[depth_tap][column_tap],
                preferred_element_type=jnp.float32,
            )
    return accumulated.reshape(out_spheres, out_columns, merged)


def clear_rims(extended, width, sphere_dim):
    device_index = lax.axis_index("depth")
    last_device = lax.axis_size("depth") - 1
    extent = extended.shape[sphere_dim]
    position = lax.broadcasted_iota(jnp.int32, (extent,), 0)
    outside = (position < width) & (device_index == 0) | (position >= extent - width) & (
        device_index == last_device
    )
    layout = [1] * extended.ndim
    layout[sphere_dim] = extent
    return jnp.where(outside.reshape(layout), jnp.zeros_like(extended), extended)


def faces_once(volume):
    extended = padded_2(volume, (("depth", 0), ("azim", 1)), 1)
    return clear_rims(extended, 1, 0)


def band_matrix(taps_camera, offsets_camera, big_count, small_count, margin, direction):
    tap_count = taps_camera.shape[1]
    big_index = lax.broadcasted_iota(jnp.int32, (1, big_count, 1, 1), 1)
    small_index = lax.broadcasted_iota(jnp.int32, (1, 1, small_count, 1), 2)
    tap_index = lax.broadcasted_iota(jnp.int32, (1, 1, 1, tap_count), 3)
    target = small_index + margin + direction * (offsets_camera[:, None, None, None] + tap_index)
    chosen = jnp.where(
        big_index == target, taps_camera[:, None, None, :], jnp.zeros((), jnp.bfloat16)
    )
    return jnp.sum(chosen, axis=3, dtype=jnp.bfloat16)


def camera_terms(
    source,
    row_resample,
    band_taps,
    col_offset,
    big_count,
    small_count,
    margin,
    direction,
    row_count,
    channels,
):
    sphere_count = source.shape[0]
    pieces = []
    for camera in range(band_taps.shape[0]):
        matrix = band_matrix(
            band_taps[camera], col_offset[camera], big_count, small_count, margin, direction
        )
        pulled = jnp.einsum("sbw,sbx->swx", matrix, source, preferred_element_type=jnp.float32)
        pulled = pulled.reshape(sphere_count, -1, row_count, channels)
        pieces.append(
            jnp.einsum(
                "shg,swhc->gwc", row_resample[camera], pulled, precision=lax.Precision.HIGHEST
            )
        )
    return jnp.concatenate(pieces, axis=-1)


def body(
    cotangent,
    pre_second,
    pre_first,
    kernel_first,
    kernel_second,
    row_resample,
    col_taps,
    band_width,
    col_offset,
):
    sphere_count, column_count, merged = cotangent.shape
    channels = kernel_first.shape[3]
    row_count = merged // channels
    mixers_second = row_mixers(kernel_second, row_count)
    mixers_first = row_mixers(kernel_first, row_count)
    second_grad = jnp.where(pre_second > 0, cotangent, jnp.zeros_like(cotangent))
    hidden_grad = transpose_conv(faces_once(second_grad), mixers_second)
    first_grad = (hidden_grad * (pre_first > 0).astype(jnp.float32)).astype(jnp.bfloat16)
    volume_grad = transpose_conv(faces_once(first_grad), mixers_first).astype(jnp.bfloat16)
    margin = SHIFT + TAPS
    band_keep = lax.broadcasted_iota(jnp.int32, col_taps.shape, 2) < band_width[:, :, None]
    band_taps = jnp.where(band_keep, col_taps, jnp.zeros_like(col_taps)).astype(jnp.bfloat16)
    extended = padded_2(volume_grad, (("azim", 1),), margin)
    partial_value = camera_terms(
        extended,
        row_resample,
        band_taps,
        col_offset,
        column_count + 2 * margin,
        column_count,
        margin,
        1,
        row_count,
        channels,
    )
    return lax.psum_scatter(partial_value, "depth", scatter_dimension=0, tiled=True)


def solution(mesh):
    placed = (
        P("depth", "azim", None),
        P("depth", "azim", None),
        P("depth", "azim", None),
        P(),
        P(),
        P(None, "depth", None, None),
        P(None, "depth", None),
        P(None, "depth"),
        P(None, "depth"),
    )
    return jax.shard_map(
        body, mesh=mesh, in_specs=placed, out_specs=P("depth", "azim", None), check_vma=False
    )
```

profile of v0, /device:TPU:4, one launch (start us, length us, event | category | flops | bytes accessed | tf_op | source)
XLA Modules:
  0.0 187.3 jit_solution(15954321492162096366)
XLA Ops:
  6.6 1.4 compare_select_fusion
  7.9 0.6 fusion.45
  8.6 3.5 %collective-permute-start = (bf16[1,64,256]{2,1,0:T(8,128)(2,1)}, bf16[1,64,256]{2,1,0:T(8,128)(2,1)S(1)}, u32[]{:S(2)}, u32[]{:S(2)}) collective-permute-start(bf16[1,64,256]{2,1,0:T(8,128)(2,1)} %get-tuple-element.31), channel_id=1, source_target_pairs={{0,64},{64,128},{128,192},{192,256},{256,320},{320,384},{384,448},... | collective-permute-start | bytes 98312 | tf_op jit(solution)/shard_map/ppermute | solution.py:16
  12.1 4.5 %collective-permute-start.1 = (bf16[1,64,256]{2,1,0:T(8,128)(2,1)}, bf16[1,64,256]{2,1,0:T(8,128)(2,1)S(1)}, u32[]{:S(2)}, u32[]{:S(2)}) collective-permute-start(bf16[1,64,256]{2,1,0:T(8,128)(2,1)} %get-tuple-element.32), channel_id=1, source_target_pairs={{64,0},{128,64},{192,128},{256,192},{320,256},{384,320},{448,384},... | collective-permute-start | bytes 98312 | tf_op jit(solution)/shard_map/ppermute | solution.py:19
  16.6 0.8 slice_bitcast_fusion.1
  17.4 0.9 slice_bitcast_fusion.2
  24.5 1.6 fusion.7
  26.1 1.9 %select_add_fusion = (bf16[8,32,8,32]{3,2,1,0:T(8,128)(2,1)}, bf16[8,32,8,32]{3,2,1,0:T(8,128)(2,1)}, bf16[8,32,8,32]{3,2,1,0:T(8,128)(2,1)}, bf16[8,32,8,32]{3,2,1,0:T(8,128)(2,1)}, bf16[8,32,8,32]{3,2,1,0:T(8,128)(2,1)}) fusion(pred[8,8]{1,0:T(8,128)(4,1)S(1)} %get-tuple-element.121, pred[8,8]{1,0:T(8,128)(4,1)S(1)} %get-tuple-element.122, ...), kind=kLoop, calls=%fused_computation.47 | loop fusion | flops 1638400 | bytes 686272 | tf_op jit(solution)/shard_map/add | solution.py:35
  28.1 2.0 %select_add_fusion.1 = (bf16[8,32,8,32]{3,2,1,0:T(8,128)(2,1)}, bf16[8,32,8,32]{3,2,1,0:T(8,128)(2,1)}, bf16[8,32,8,32]{3,2,1,0:T(8,128)(2,1)}, bf16[8,32,8,32]{3,2,1,0:T(8,128)(2,1)}, bf16[8,32,8,32]{3,2,1,0:T(8,128)(2,1)}) fusion(pred[8,8]{1,0:T(8,128)(4,1)S(1)} %get-tuple-element.121, pred[8,8]{1,0:T(8,128)(4,1)S(1)} %get-tuple-element.122, ...), kind=kLoop, calls=%fused_computation.48 | loop fusion | flops 1638400 | bytes 686272 | tf_op jit(solution)/shard_map/add | solution.py:35
  30.1 1.9 %select_add_fusion.2 = (bf16[8,32,8,32]{3,2,1,0:T(8,128)(2,1)}, bf16[8,32,8,32]{3,2,1,0:T(8,128)(2,1)}, bf16[8,32,8,32]{3,2,1,0:T(8,128)(2,1)}, bf16[8,32,8,32]{3,2,1,0:T(8,128)(2,1)}, bf16[8,32,8,32]{3,2,1,0:T(8,128)(2,1)}) fusion(pred[8,8]{1,0:T(8,128)(4,1)S(1)} %get-tuple-element.121, pred[8,8]{1,0:T(8,128)(4,1)S(1)} %get-tuple-element.122, ...), kind=kLoop, calls=%fused_computation.49 | loop fusion | flops 1638400 | bytes 686272 | tf_op jit(solution)/shard_map/add | solution.py:35
  32.0 1.9 %select_add_fusion.3 = (bf16[8,32,8,32]{3,2,1,0:T(8,128)(2,1)S(1)}, bf16[8,32,8,32]{3,2,1,0:T(8,128)(2,1)S(1)}, bf16[8,32,8,32]{3,2,1,0:T(8,128)(2,1)}) fusion(pred[8,8]{1,0:T(8,128)(4,1)S(1)} %get-tuple-element.121, pred[8,8]{1,0:T(8,128)(4,1)S(1)} %get-tuple-element.122, pred[8,8]{1,0:T(8,128)(4,1)} %copy-done.22, bf16[32,32]{1,0:T(8,128)(2,1)S(1)} %copy.252, ...), kind=kLoop, calls=%fused_computation.50 | loop fusion | flops 983040 | bytes 411840 | tf_op jit(solution)/shard_map/add | solution.py:35
  33.9 0.6 pad_maximum_fusion.7
  34.6 1.9 %collective-permute-start.2 = (bf16[18,1,256]{2,1,0:T(2,128)(2,1)}, bf16[18,1,256]{2,1,0:T(2,128)(2,1)}, u32[]{:S(2)}, u32[]{:S(2)}) collective-permute-start(bf16[18,1,256]{2,1,0:T(2,128)(2,1)} %get-tuple-element.25), channel_id=1, source_target_pairs={{0,1},{1,2},{2,3},{3,4},{4,5},{5,6},{6,7},{7,8},{8,9},{9,10},{10,1... | collective-permute-start | bytes 27656 | tf_op jit(solution)/shard_map/ppermute | solution.py:16
  36.5 5.1 %collective-permute-start.3 = (bf16[18,1,256]{2,1,0:T(2,128)(2,1)}, bf16[18,1,256]{2,1,0:T(2,128)(2,1)}, u32[]{:S(2)}, u32[]{:S(2)}) collective-permute-start(bf16[18,1,256]{2,1,0:T(2,128)(2,1)} %get-tuple-element.26), channel_id=1, source_target_pairs={{1,0},{2,1},{3,2},{4,3},{5,4},{6,5},{7,6},{8,7},{9,8},{10,9},{11,1... | collective-permute-start | bytes 27656 | tf_op jit(solution)/shard_map/ppermute | solution.py:19
  41.7 0.7 copy.264
  42.4 2.1 %add.760 = bf16[256,256]{1,0:T(8,128)(2,1)} reshape(bf16[8,32,8,32]{3,2,1,0:T(8,128)(2,1)} %get-tuple-element.108) | data formatting | bytes 262144 | tf_op jit(solution)/shard_map/add | solution.py:35
  44.5 2.1 %add.763 = bf16[256,256]{1,0:T(8,128)(2,1)} reshape(bf16[8,32,8,32]{3,2,1,0:T(8,128)(2,1)} %get-tuple-element.92) | data formatting | bytes 262144 | tf_op jit(solution)/shard_map/add | solution.py:35
  46.6 2.1 %add.767 = bf16[256,256]{1,0:T(8,128)(2,1)} reshape(bf16[8,32,8,32]{3,2,1,0:T(8,128)(2,1)} %get-tuple-element.93) | data formatting | bytes 262144 | tf_op jit(solution)/shard_map/add | solution.py:35
  48.7 2.1 %add.771 = bf16[256,256]{1,0:T(8,128)(2,1)} reshape(bf16[8,32,8,32]{3,2,1,0:T(8,128)(2,1)} %get-tuple-element.94) | data formatting | bytes 262144 | tf_op jit(solution)/shard_map/add | solution.py:35
  50.8 2.1 %add.775 = bf16[256,256]{1,0:T(8,128)(2,1)} reshape(bf16[8,32,8,32]{3,2,1,0:T(8,128)(2,1)} %get-tuple-element.95) | data formatting | bytes 262144 | tf_op jit(solution)/shard_map/add | solution.py:35
  52.9 2.1 %add.779 = bf16[256,256]{1,0:T(8,128)(2,1)} reshape(bf16[8,32,8,32]{3,2,1,0:T(8,128)(2,1)} %get-tuple-element.97) | data formatting | bytes 262144 | tf_op jit(solution)/shard_map/add | solution.py:35
  55.0 2.1 %add.783 = bf16[256,256]{1,0:T(8,128)(2,1)} reshape(bf16[8,32,8,32]{3,2,1,0:T(8,128)(2,1)} %get-tuple-element.98) | data formatting | bytes 262144 | tf_op jit(solution)/shard_map/add | solution.py:35
  57.1 2.1 %add.787 = bf16[256,256]{1,0:T(8,128)(2,1)} reshape(bf16[8,32,8,32]{3,2,1,0:T(8,128)(2,1)} %get-tuple-element.99) | data formatting | bytes 262144 | tf_op jit(solution)/shard_map/add | solution.py:35
  59.2 1.4 add.791
  60.7 1.0 maximum_select_fusion
  66.9 1.9 %collective-permute-start.4 = (bf16[1,64,256]{2,1,0:T(8,128)(2,1)S(1)}, bf16[1,64,256]{2,1,0:T(8,128)(2,1)S(1)}, u32[]{:S(2)}, u32[]{:S(2)}) collective-permute-start(bf16[1,64,256]{2,1,0:T(8,128)(2,1)S(1)} %get-tuple-element.29), channel_id=1, source_target_pairs={{0,64},{64,128},{128,192},{192,256},{256,320},{320,384},{384,448},... | collective-permute-start | bytes 98312 | tf_op jit(solution)/shard_map/ppermute | solution.py:16
  68.8 6.2 %collective-permute-start.5 = (bf16[1,64,256]{2,1,0:T(8,128)(2,1)S(1)}, bf16[1,64,256]{2,1,0:T(8,128)(2,1)S(1)}, u32[]{:S(2)}, u32[]{:S(2)}) collective-permute-start(bf16[1,64,256]{2,1,0:T(8,128)(2,1)S(1)} %get-tuple-element.30), channel_id=1, source_target_pairs={{64,0},{128,64},{192,128},{256,192},{320,256},{384,320},{448,384},... | collective-permute-start | bytes 98312 | tf_op jit(solution)/shard_map/ppermute | solution.py:19
  75.1 2.3 %fusion.6 = bf16[16,128,64]{1,2,0:T(8,128)(2,1)} fusion(s32[16,64,8]{2,1,0:T(8,128)S(1)} %get-tuple-element.114, bf16[16,8]{1,0:T(8,128)(2,1)S(1)} %copy.264), kind=kLoop, calls=%fused_computation.10 | loop fusion | flops 3014656 | bytes 295168 | tf_op jit(solution)/shard_map/reduce_sum | solution.py:89
  77.5 0.6 pad_maximum_fusion.4
  78.1 1.9 %collective-permute-start.6 = (bf16[18,1,256]{2,1,0:T(2,128)(2,1)}, bf16[18,1,256]{2,1,0:T(2,128)(2,1)}, u32[]{:S(2)}, u32[]{:S(2)}) collective-permute-start(bf16[18,1,256]{2,1,0:T(2,128)(2,1)} %get-tuple-element.23), channel_id=1, source_target_pairs={{0,1},{1,2},{2,3},{3,4},{4,5},{5,6},{6,7},{7,8},{8,9},{9,10},{10,1... | collective-permute-start | bytes 27656 | tf_op jit(solution)/shard_map/ppermute | solution.py:16
  80.1 5.1 %collective-permute-start.7 = (bf16[18,1,256]{2,1,0:T(2,128)(2,1)}, bf16[18,1,256]{2,1,0:T(2,128)(2,1)}, u32[]{:S(2)}, u32[]{:S(2)}) collective-permute-start(bf16[18,1,256]{2,1,0:T(2,128)(2,1)} %get-tuple-element.24), channel_id=1, source_target_pairs={{1,0},{2,1},{3,2},{4,3},{5,4},{6,5},{7,6},{8,7},{9,8},{10,9},{11,1... | collective-permute-start | bytes 27656 | tf_op jit(solution)/shard_map/ppermute | solution.py:19
  85.2 2.3 %fusion.5 = bf16[16,128,64]{1,2,0:T(8,128)(2,1)} fusion(s32[16,64,8]{2,1,0:T(8,128)S(1)} %get-tuple-element.115, bf16[16,8]{1,0:T(8,128)(2,1)S(1)} %copy.267), kind=kLoop, calls=%fused_computation.9 | loop fusion | flops 3014656 | bytes 295168 | tf_op jit(solution)/shard_map/reduce_sum | solution.py:89
  88.0 1.0 add.810
  89.1 1.5 add.826
  90.9 1.4 add.818
  92.4 1.4 add.795
  93.8 1.4 add.798
  96.0 1.0 maximum_select_fusion.1
  100.8 1.9 %collective-permute-start.8 = (bf16[16,32,256]{2,1,0:T(8,128)(2,1)S(1)}, bf16[16,32,256]{2,1,0:T(8,128)(2,1)S(1)}, u32[]{:S(2)}, u32[]{:S(2)}) collective-permute-start(bf16[16,32,256]{2,1,0:T(8,128)(2,1)S(1)} %get-tuple-element.27), channel_id=1, source_target_pairs={{0,1},{1,2},{2,3},{3,4},{4,5},{5,6},{6,7},{7,8},{8,9},{9,10},{10,1... | collective-permute-start | bytes 786440 | tf_op jit(solution)/shard_map/ppermute | solution.py:16
  102.7 6.9 %collective-permute-start.9 = (bf16[16,32,256]{2,1,0:T(8,128)(2,1)S(1)}, bf16[16,32,256]{2,1,0:T(8,128)(2,1)S(1)}, u32[]{:S(2)}, u32[]{:S(2)}) collective-permute-start(bf16[16,32,256]{2,1,0:T(8,128)(2,1)S(1)} %get-tuple-element.28), channel_id=1, source_target_pairs={{1,0},{2,1},{3,2},{4,3},{5,4},{6,5},{7,6},{8,7},{9,8},{10,9},{11,1... | collective-permute-start | bytes 786440 | tf_op jit(solution)/shard_map/ppermute | solution.py:19
  109.6 1.9 fusion.4
  111.7 1.8 collective-permute-done.9
  114.0 2.4 %fusion.20 = f32[8,64,32]{1,0,2:T(8,128)S(1)} fusion(f32[16,64,8,32]{1,3,2,0:T(8,128)S(1)} %bitcast.374, f32[4,16,8,8]{1,3,2,0:T(8,128)S(1)} %copy-done.16), kind=kOutput, calls=%fused_computation.38 | convolution fusion | flops 25165824 | bytes 2195456 | tf_op jit(solution)/shard_map/shg,swhc->gwc/dot_general | solution.py:113
  116.9 2.4 %fusion.23 = f32[8,64,32]{1,0,2:T(8,128)S(1)} fusion(f32[16,64,8,32]{1,3,2,0:T(8,128)S(1)} %bitcast.375, f32[4,16,8,8]{1,3,2,0:T(8,128)S(1)} %copy-done.16), kind=kOutput, calls=%fused_computation.39 | convolution fusion | flops 25165824 | bytes 2195456 | tf_op jit(solution)/shard_map/shg,swhc->gwc/dot_general | solution.py:113
  119.8 2.4 %fusion.26 = f32[8,64,32]{1,0,2:T(8,128)S(1)} fusion(f32[16,64,8,32]{1,3,2,0:T(8,128)S(1)} %bitcast.376, f32[4,16,8,8]{1,3,2,0:T(8,128)S(1)} %copy-done.16), kind=kOutput, calls=%fused_computation.40 | convolution fusion | flops 25165824 | bytes 2195456 | tf_op jit(solution)/shard_map/shg,swhc->gwc/dot_general | solution.py:113
  122.6 2.4 %fusion.17 = f32[8,64,32]{1,0,2:T(8,128)S(1)} fusion(f32[16,64,8,32]{1,3,2,0:T(8,128)S(1)} %bitcast.373, f32[4,16,8,8]{1,3,2,0:T(8,128)S(1)} %copy-done.16), kind=kOutput, calls=%fused_computation.37 | convolution fusion | flops 25165824 | bytes 2195456 | tf_op jit(solution)/shard_map/shg,swhc->gwc/dot_general | solution.py:113
  125.1 0.9 copy.273
  126.0 54.4 %reduce-scatter.2.cloned.1.call-done = f32[1,64,128]{2,1,0:T(8,128)} async-done(((f32[8,64,128]{2,1,0:T(8,128)}), f32[1,64,128]{2,1,0:T(8,128)}) %reduce-scatter.2.cloned.1.call-update) | async-done | bytes 32784 | tf_op jit(solution)/shard_map/reduce_scatter | solution.py:156
  (168 shorter events, 18.7 us)
Async XLA Ops:
  6.5 11.8 %copy-start.15 = (bf16[3,3,3,32,32]{4,3,2,1,0:T(8,128)(2,1)S(1)}, bf16[3,3,3,32,32]{4,3,2,1,0:T(8,128)(2,1)}, u32[]{:S(2)}) copy-start(bf16[3,3,3,32,32]{4,3,2,1,0:T(8,128)(2,1)} %param.13) | copy-start | bytes 165892
  6.5 11.8 %copy-start.25 = (s32[4,16]{1,0:T(4,128)S(1)}, s32[4,16]{1,0:T(4,128)}, u32[]{:S(2)}) copy-start(s32[4,16]{1,0:T(4,128)} %param.17) | copy-start | bytes 772
  6.5 11.9 %copy-start.26 = (s32[4,16]{1,0:T(4,128)S(1)}, s32[4,16]{1,0:T(4,128)}, u32[]{:S(2)}) copy-start(s32[4,16]{1,0:T(4,128)} %param.16) | copy-start | bytes 772
  6.5 11.9 %copy-start.21 = (f32[4,16,8]{1,2,0:T(8,128)S(1)}, f32[4,16,8]{1,2,0:T(8,128)}, u32[]{:S(2)}) copy-start(f32[4,16,8]{1,2,0:T(8,128)} %param.15) | copy-start | bytes 6148
  6.5 173.9 %reduce-scatter.2.cloned.1.call-start = ((), (), s32[]{:S(2)}) async-start(), calls=%async_computation.1 | async-start | bytes 294912 | tf_op jit(solution)/shard_map/reduce_scatter | solution.py:156
  8.6 25.3 %collective-permute-start = (bf16[1,64,256]{2,1,0:T(8,128)(2,1)}, bf16[1,64,256]{2,1,0:T(8,128)(2,1)S(1)}, u32[]{:S(2)}, u32[]{:S(2)}) collective-permute-start(bf16[1,64,256]{2,1,0:T(8,128)(2,1)} %get-tuple-element.31), channel_id=1, source_target_pairs={{0,64},{64,128},{128,192},{192,256},{256,320},{320,384},{384,448},... | collective-permute-start | bytes 98312 | tf_op jit(solution)/shard_map/ppermute | solution.py:16
  12.1 21.9 %collective-permute-start.1 = (bf16[1,64,256]{2,1,0:T(8,128)(2,1)}, bf16[1,64,256]{2,1,0:T(8,128)(2,1)S(1)}, u32[]{:S(2)}, u32[]{:S(2)}) collective-permute-start(bf16[1,64,256]{2,1,0:T(8,128)(2,1)} %get-tuple-element.32), channel_id=1, source_target_pairs={{64,0},{128,64},{192,128},{256,192},{320,256},{384,320},{448,384},... | collective-permute-start | bytes 98312 | tf_op jit(solution)/shard_map/ppermute | solution.py:19
  18.4 11.7 %copy-start.22 = (pred[8,8]{1,0:T(8,128)(4,1)}, pred[8,8]{1,0:T(8,128)(4,1)S(1)}, u32[]{:S(2)}) copy-start(pred[8,8]{1,0:T(8,128)(4,1)S(1)} %iota_compare_fusion.7) | copy-start | bytes 196
  33.9 21.1 %copy-start.17 = (bf16[1,64,256]{2,1,0:T(8,128)(2,1)}, bf16[1,64,256]{2,1,0:T(8,128)(2,1)S(1)}, u32[]{:S(2)}) copy-start(bf16[1,64,256]{2,1,0:T(8,128)(2,1)S(1)} %collective-permute-done) | copy-start | bytes 98308
  33.9 21.1 %copy-start.18 = (bf16[1,64,256]{2,1,0:T(8,128)(2,1)}, bf16[1,64,256]{2,1,0:T(8,128)(2,1)S(1)}, u32[]{:S(2)}) copy-start(bf16[1,64,256]{2,1,0:T(8,128)(2,1)S(1)} %collective-permute-done.1) | copy-start | bytes 98308
  34.6 26.1 %collective-permute-start.2 = (bf16[18,1,256]{2,1,0:T(2,128)(2,1)}, bf16[18,1,256]{2,1,0:T(2,128)(2,1)}, u32[]{:S(2)}, u32[]{:S(2)}) collective-permute-start(bf16[18,1,256]{2,1,0:T(2,128)(2,1)} %get-tuple-element.25), channel_id=1, source_target_pairs={{0,1},{1,2},{2,3},{3,4},{4,5},{5,6},{6,7},{7,8},{8,9},{9,10},{10,1... | collective-permute-start | bytes 27656 | tf_op jit(solution)/shard_map/ppermute | solution.py:16
  36.5 24.2 %collective-permute-start.3 = (bf16[18,1,256]{2,1,0:T(2,128)(2,1)}, bf16[18,1,256]{2,1,0:T(2,128)(2,1)}, u32[]{:S(2)}, u32[]{:S(2)}) collective-permute-start(bf16[18,1,256]{2,1,0:T(2,128)(2,1)} %get-tuple-element.26), channel_id=1, source_target_pairs={{1,0},{2,1},{3,2},{4,3},{5,4},{6,5},{7,6},{8,7},{9,8},{10,9},{11,1... | collective-permute-start | bytes 27656 | tf_op jit(solution)/shard_map/ppermute | solution.py:19
  61.7 0.9 copy-start.6
  61.7 1.2 copy-start.14
  62.6 0.9 copy-start.13
  62.9 0.9 copy-start.12
  63.5 0.9 copy-start.11
  63.8 0.9 copy-start.10
  64.5 0.9 copy-start.9
  64.8 0.9 copy-start.8
  65.7 1.0 copy-start.5
  66.0 11.4 %copy-start.24 = (bf16[16,8]{0,1:T(8,128)(2,1)S(1)}, bf16[16,8]{0,1:T(8,128)(2,1)}, u32[]{:S(2)}) copy-start(bf16[16,8]{0,1:T(8,128)(2,1)} %get-tuple-element.89) | copy-start | bytes 772
  66.3 21.3 %copy-start.23 = (bf16[16,8]{0,1:T(8,128)(2,1)S(1)}, bf16[16,8]{0,1:T(8,128)(2,1)}, u32[]{:S(2)}) copy-start(bf16[16,8]{0,1:T(8,128)(2,1)} %get-tuple-element.88) | copy-start | bytes 772
  66.9 10.6 %collective-permute-start.4 = (bf16[1,64,256]{2,1,0:T(8,128)(2,1)S(1)}, bf16[1,64,256]{2,1,0:T(8,128)(2,1)S(1)}, u32[]{:S(2)}, u32[]{:S(2)}) collective-permute-start(bf16[1,64,256]{2,1,0:T(8,128)(2,1)S(1)} %get-tuple-element.29), channel_id=1, source_target_pairs={{0,64},{64,128},{128,192},{192,256},{256,320},{320,384},{384,448},... | collective-permute-start | bytes 98312 | tf_op jit(solution)/shard_map/ppermute | solution.py:16
  68.8 8.7 %collective-permute-start.5 = (bf16[1,64,256]{2,1,0:T(8,128)(2,1)S(1)}, bf16[1,64,256]{2,1,0:T(8,128)(2,1)S(1)}, u32[]{:S(2)}, u32[]{:S(2)}) collective-permute-start(bf16[1,64,256]{2,1,0:T(8,128)(2,1)S(1)} %get-tuple-element.30), channel_id=1, source_target_pairs={{64,0},{128,64},{192,128},{256,192},{320,256},{384,320},{448,384},... | collective-permute-start | bytes 98312 | tf_op jit(solution)/shard_map/ppermute | solution.py:19
  77.4 13.2 %copy-start = (bf16[8,32,8,32]{3,2,1,0:T(8,128)(2,1)S(1)}, bf16[8,32,8,32]{3,2,1,0:T(8,128)(2,1)}, u32[]{:S(2)}) copy-start(bf16[8,32,8,32]{3,2,1,0:T(8,128)(2,1)} %get-tuple-element.96) | copy-start | bytes 393220
  77.5 10.2 %copy-start.19 = (bf16[1,64,256]{2,1,0:T(8,128)(2,1)}, bf16[1,64,256]{2,1,0:T(8,128)(2,1)S(1)}, u32[]{:S(2)}) copy-start(bf16[1,64,256]{2,1,0:T(8,128)(2,1)S(1)} %collective-permute-done.4) | copy-start | bytes 98308
  77.5 10.2 %copy-start.20 = (bf16[1,64,256]{2,1,0:T(8,128)(2,1)}, bf16[1,64,256]{2,1,0:T(8,128)(2,1)S(1)}, u32[]{:S(2)}) copy-start(bf16[1,64,256]{2,1,0:T(8,128)(2,1)S(1)} %collective-permute-done.5) | copy-start | bytes 98308
  78.1 17.9 %collective-permute-start.6 = (bf16[18,1,256]{2,1,0:T(2,128)(2,1)}, bf16[18,1,256]{2,1,0:T(2,128)(2,1)}, u32[]{:S(2)}, u32[]{:S(2)}) collective-permute-start(bf16[18,1,256]{2,1,0:T(2,128)(2,1)} %get-tuple-element.23), channel_id=1, source_target_pairs={{0,1},{1,2},{2,3},{3,4},{4,5},{5,6},{6,7},{7,8},{8,9},{9,10},{10,1... | collective-permute-start | bytes 27656 | tf_op jit(solution)/shard_map/ppermute | solution.py:16
  80.1 16.0 %collective-permute-start.7 = (bf16[18,1,256]{2,1,0:T(2,128)(2,1)}, bf16[18,1,256]{2,1,0:T(2,128)(2,1)}, u32[]{:S(2)}, u32[]{:S(2)}) collective-permute-start(bf16[18,1,256]{2,1,0:T(2,128)(2,1)} %get-tuple-element.24), channel_id=1, source_target_pairs={{1,0},{2,1},{3,2},{4,3},{5,4},{6,5},{7,6},{8,7},{9,8},{10,9},{11,1... | collective-permute-start | bytes 27656 | tf_op jit(solution)/shard_map/ppermute | solution.py:19
  88.0 7.2 %copy-start.2 = (bf16[8,32,8,32]{3,2,1,0:T(8,128)(2,1)S(1)}, bf16[8,32,8,32]{3,2,1,0:T(8,128)(2,1)}, u32[]{:S(2)}) copy-start(bf16[8,32,8,32]{3,2,1,0:T(8,128)(2,1)} %get-tuple-element.104) | copy-start | bytes 393220
  89.1 6.6 %copy-start.1 = (bf16[8,32,8,32]{3,2,1,0:T(8,128)(2,1)S(1)}, bf16[8,32,8,32]{3,2,1,0:T(8,128)(2,1)}, u32[]{:S(2)}) copy-start(bf16[8,32,8,32]{3,2,1,0:T(8,128)(2,1)} %get-tuple-element.105) | copy-start | bytes 393220
  98.3 0.9 copy-start.7
  100.4 13.1 %copy-start.3 = (bf16[16,128,64]{1,2,0:T(8,128)(2,1)S(1)}, bf16[16,128,64]{1,2,0:T(8,128)(2,1)}, u32[]{:S(2)}) copy-start(bf16[16,128,64]{1,2,0:T(8,128)(2,1)} %fusion.6) | copy-start | bytes 786436
  100.8 10.9 %collective-permute-start.8 = (bf16[16,32,256]{2,1,0:T(8,128)(2,1)S(1)}, bf16[16,32,256]{2,1,0:T(8,128)(2,1)S(1)}, u32[]{:S(2)}, u32[]{:S(2)}) collective-permute-start(bf16[16,32,256]{2,1,0:T(8,128)(2,1)S(1)} %get-tuple-element.27), channel_id=1, source_target_pairs={{0,1},{1,2},{2,3},{3,4},{4,5},{5,6},{6,7},{7,8},{8,9},{9,10},{10,1... | collective-permute-start | bytes 786440 | tf_op jit(solution)/shard_map/ppermute | solution.py:16
  102.7 10.8 %collective-permute-start.9 = (bf16[16,32,256]{2,1,0:T(8,128)(2,1)S(1)}, bf16[16,32,256]{2,1,0:T(8,128)(2,1)S(1)}, u32[]{:S(2)}, u32[]{:S(2)}) collective-permute-start(bf16[16,32,256]{2,1,0:T(8,128)(2,1)S(1)} %get-tuple-element.28), channel_id=1, source_target_pairs={{1,0},{2,1},{3,2},{4,3},{5,4},{6,5},{7,6},{8,7},{9,8},{10,9},{11,1... | collective-permute-start | bytes 786440 | tf_op jit(solution)/shard_map/ppermute | solution.py:19
  109.6 4.4 %copy-start.16 = (f32[4,16,8,8]{1,3,2,0:T(8,128)S(1)}, f32[4,16,8,8]{1,3,2,0:T(8,128)}, u32[]{:S(2)}) copy-start(f32[4,16,8,8]{1,3,2,0:T(8,128)} %param.14) | copy-start | bytes 49156
  111.5 4.9 %copy-start.4 = (bf16[16,128,64]{1,2,0:T(8,128)(2,1)S(1)}, bf16[16,128,64]{1,2,0:T(8,128)(2,1)}, u32[]{:S(2)}) copy-start(bf16[16,128,64]{1,2,0:T(8,128)(2,1)} %fusion.5) | copy-start | bytes 786436
Sparse Core Ops, SparseCore 0:
  126.2 54.2 reduce-scatter.1
where the time goes:
time: 189 us; the launch traced here: 187 us
  waiting for transfers between devices  56.4 us (30%)
  local copies, waits for them, and re-layouts  39.5 us (21%)
  starting transfers between devices  39 us (21%)
  other arithmetic  21.4 us (11%)
  matrix products  16.9 us (9%)
  between operations  14.1 us (7%)
    reduce_scatter x1, waiting for transfers between devices, body(): lax.psum_scatter(partial_value, 'depth', scatter_dimension=0, tiled=True)  54.4 us
    ppermute x5, starting transfers between devices, padded_2(): lax.ppermute(lax.slice_in_dim(block, 0, width, axis=dim), axis, backward)  27.9 us
    add x18, local copies, waits for them, and re-layouts, row_mixers(): mixed + jnp.where(row_in == row_out + 1 - row_tap, block, jnp.zeros((), j...  26.5 us
    ppermute x5, starting transfers between devices, padded_2(): lax.ppermute(lax.slice_in_dim(block, block.shape[dim] - width, None, axis...  11.1 us
    dot_general x4, matrix products, camera_terms(): jnp.einsum('shg,swhc->gwc', row_resample[camera], pulled, precision=lax.P...  9.6 us
    reduce_sum x4, other arithmetic, band_matrix(): return jnp.sum(chosen, axis=3, dtype=jnp.bfloat16)  8.17 us
    add x4, other arithmetic, row_mixers(): mixed + jnp.where(row_in == row_out + 1 - row_tap, block, jnp.zeros((), j...  7.77 us
    transpose x58, local copies, waits for them, and re-layouts, row_mixers(): block = kernel[depth_tap, column_tap, row_tap].T[None, :, None, :]  6.6 us
  transfers between devices with their start and end apart: 11, of which 3 were waited for; matrix products, arithmetic and copies ran while one was open for 27% of the time, Pallas kernels for 0%

commit v1 on v0

v1 whole, which is shorter than its diff:
```python
import numpy as np
import jax
import jax.numpy as jnp
from jax import lax
from jax.experimental import pallas as pl
from jax.experimental.pallas import tpu as pltpu
from jax.sharding import PartitionSpec as P

TAPS = 8
SHIFT = 24
NS = 16
NW = 64
ROWS = 8
C = 32
RC = ROWS * C
CAMS = 4
ND = 8
F32 = jnp.float32
BF16 = jnp.bfloat16
CH1 = 6
CH2 = 8


def stage_select():
    sel = np.zeros((160, 1024), np.float32)

    def at(array, sphere, column):
        part = 2 * array + (0 if column < 16 else 1)
        return 256 * part + 16 * sphere + column % 16

    for s in range(NS):
        sel[s, at(0, s, 62)] = 1
        sel[16 + s, at(0, s, 63)] = 1
        sel[32 + s, at(1, s, 63)] = 1
        sel[48 + s, at(0, s, 0)] = 1
        sel[64 + s, at(0, s, 1)] = 1
        sel[80 + s, at(1, s, 0)] = 1
    corners = ((96, 14, 62), (112, 14, 0), (128, 0, 62), (144, 0, 0))
    for base, sphere, column in corners:
        for i in range(4):
            sel[base + i, at(0, sphere + i // 2, column + i % 2)] = 1
        pf_sphere = 15 if sphere == 14 else 0
        pf_column = 63 if column == 62 else 0
        sel[base + 4, at(1, pf_sphere, pf_column)] = 1
    return sel


def edge_expand():
    mat = np.zeros((20 + 20 + 18, 16, 160), np.float32)
    for e in range(20):
        if e < 2:
            left, right = [96 + 2 * e, 97 + 2 * e], [112 + 2 * e, 113 + 2 * e]
        elif e < 18:
            left, right = [e - 2, 16 + e - 2], [48 + e - 2, 64 + e - 2]
        else:
            f = e - 18
            left, right = [128 + 2 * f, 129 + 2 * f], [144 + 2 * f, 145 + 2 * f]
        mat[e, 0, left[1]] = 1
        mat[e, 15, right[0]] = 1
        mat[20 + e, 0, left[0]] = 1
        mat[20 + e, 15, right[1]] = 1
    for f in range(18):
        left = 100 if f == 0 else 132 if f == 17 else 32 + f - 1
        right = 116 if f == 0 else 148 if f == 17 else 80 + f - 1
        mat[40 + f, 0, left] = 1
        mat[40 + f, 15, right] = 1
    return mat.reshape(-1, 160)


def row_place():
    place = np.zeros((ROWS, 3, C, ROWS, C), np.float32)
    for r_in in range(ROWS):
        for tap in range(3):
            r_out = r_in - 1 + tap
            if 0 <= r_out < ROWS:
                place[r_in, tap, np.arange(C), r_out, np.arange(C)] = 1
    return place.reshape(ROWS, 3 * C, RC)


def lane_rows():
    out = np.zeros((CAMS, ROWS, ROWS, RC), np.float32)
    lane = np.arange(RC)
    for k in range(CAMS):
        row = 4 * (lane // 128) + ((lane % 128) // 32 - k) % 4
        out[k, :, row, lane] = 1
    return out.reshape(CAMS, ROWS * ROWS, RC)


def sphere_lanes():
    out = np.zeros((NS, NS * NW), np.float32)
    out[np.arange(NS * NW) // NW, np.arange(NS * NW)] = 1
    return out


def kernel(
    cot_h, pre2_h, pre1_h, k1_h, k2_h, rr_h, taps_h, width_h, off_h,
    sel_h, exp_h, place_h, lrow_h, slane_h,
    out_ref,
    cot, pre2, pfx, g2x, kk, rr, taps, width, off,
    sel, expm, place, lrow, slane,
    stage, hc, s1, s2, pft, edges, kc, w2, w1, lbuf, rt, band, vol, ymix, zbuf, rbuf,
    in_sem, fs_sem, fr_sem, bs_sem, br_sem,
):
    d = lax.axis_index("depth")
    a = lax.axis_index("azim")
    na = lax.axis_size("azim")
    a_up = lax.rem(a + 1, na)
    a_dn = lax.rem(a + na - 1, na)

    def load(i, src, dst):
        copy = pltpu.make_async_copy(src, dst, in_sem.at[i])
        copy.start()
        return copy

    ld_pre1 = load(2, pre1_h, pfx.at[pl.ds(1, NS)])
    ld_cot = load(0, cot_h, cot)
    ld_pre2 = load(1, pre2_h, pre2)
    ld_sel = load(3, sel_h, sel)
    ld_k2 = load(4, k2_h, kk.at[0])
    ld_k1 = load(5, k1_h, kk.at[1])
    ld_place = load(6, place_h, place)
    ld_rr = load(7, rr_h, rr)
    ld_lrow = load(8, lrow_h, lrow)
    ld_taps = load(9, taps_h, taps)
    ld_width = load(10, width_h, width)
    ld_off = load(11, off_h, off)
    ld_slane = load(12, slane_h, slane)
    ld_exp = load(13, exp_h, expm)

    barrier = pltpu.get_barrier_semaphore()
    for j in range(ND):
        t = lax.rem(d + j, ND)
        for col in (a_dn, a, a_up):
            if j == 0 and col is a:
                continue
            pl.semaphore_signal(
                barrier, inc=1, device_id={"depth": t, "azim": col},
                device_id_type=pl.DeviceIdType.MESH,
            )

    @pl.when(d == 0)
    def _():
        g2x[0:2] = jnp.zeros((2, NW, RC), BF16)
        pfx[0:1] = jnp.zeros((1, NW, RC), BF16)
        hc[96:128] = jnp.zeros((32, RC), BF16)

    @pl.when(d == ND - 1)
    def _():
        g2x[18:20] = jnp.zeros((2, NW, RC), BF16)
        pfx[17:18] = jnp.zeros((1, NW, RC), BF16)
        hc[128:160] = jnp.zeros((32, RC), BF16)

    ld_cot.wait()
    ld_pre2.wait()
    g2x[2:18] = jnp.where(pre2[...] > 0, cot[...], jnp.zeros((), BF16))
    ld_pre1.wait()
    ld_sel.wait()
    acc = jnp.zeros((160, RC), F32)
    for part, ref in enumerate((g2x.at[2:18, 0:16], g2x.at[2:18, 48:64],
                                pfx.at[1:17, 0:16], pfx.at[1:17, 48:64])):
        acc = acc + jnp.dot(
            sel[:, 256 * part : 256 * part + 256], ref[...].reshape(256, RC),
            preferred_element_type=F32,
        )
    stage[...] = acc.astype(BF16)

    pl.semaphore_wait(barrier, 3 * ND - 1)

    def remote(i, src, dst, dep, col):
        return pltpu.make_async_remote_copy(
            src_ref=src, dst_ref=dst, send_sem=fs_sem.at[i], recv_sem=fr_sem.at[i],
            device_id={"depth": dep, "azim": col}, device_id_type=pl.DeviceIdType.MESH,
        )

    up = jnp.minimum(d + 1, ND - 1)
    dn = jnp.maximum(d - 1, 0)
    to_up = [
        remote(0, g2x.at[pl.ds(16, 2)], g2x.at[pl.ds(0, 2)], up, a),
        remote(1, pfx.at[pl.ds(16, 1)], pfx.at[pl.ds(0, 1)], up, a),
        remote(2, stage.at[pl.ds(96, 16)], hc.at[pl.ds(96, 16)], up, a_up),
        remote(3, stage.at[pl.ds(112, 16)], hc.at[pl.ds(112, 16)], up, a_dn),
    ]
    to_dn = [
        remote(4, g2x.at[pl.ds(2, 2)], g2x.at[pl.ds(18, 2)], dn, a),
        remote(5, pfx.at[pl.ds(1, 1)], pfx.at[pl.ds(17, 1)], dn, a),
        remote(6, stage.at[pl.ds(128, 16)], hc.at[pl.ds(128, 16)], dn, a_up),
        remote(7, stage.at[pl.ds(144, 16)], hc.at[pl.ds(144, 16)], dn, a_dn),
    ]
    sides = [
        remote(8, stage.at[pl.ds(0, 48)], hc.at[pl.ds(0, 48)], d, a_up),
        remote(9, stage.at[pl.ds(48, 48)], hc.at[pl.ds(48, 48)], d, a_dn),
    ]
    for copy in sides:
        copy.start()

    @pl.when(d < ND - 1)
    def _():
        for copy in to_up:
            copy.start()

    @pl.when(d > 0)
    def _():
        for copy in to_dn:
            copy.start()

    ld_k2.wait()
    ld_k1.wait()
    ld_place.wait()
    eye = (
        lax.broadcasted_iota(jnp.int32, (C, C), 0) == lax.broadcasted_iota(jnp.int32, (C, C), 1)
    ).astype(BF16)
    for layer, w in enumerate((w2, w1)):
        for pair in range(9):
            kc[layer, pl.ds(pair * C, C)] = lax.dot_general(
                eye, kk[layer, pair], (((1,), (1,)), ((), ())), preferred_element_type=F32
            ).astype(BF16)
        for r_in in range(ROWS):
            mixed = jnp.dot(kc[layer], place[r_in], preferred_element_type=F32)
            w[:, pl.ds(r_in * C, C), :] = mixed.astype(BF16).reshape(9, C, RC)

    ld_rr.wait()
    ld_lrow.wait()
    eye16 = (
        lax.broadcasted_iota(jnp.int32, (NS, NS), 0) == lax.broadcasted_iota(jnp.int32, (NS, NS), 1)
    ).astype(BF16)
    own_row = (
        lax.broadcasted_iota(jnp.int32, (ROWS * NS, ROWS * ROWS), 0) // NS
        == lax.broadcasted_iota(jnp.int32, (ROWS * NS, ROWS * ROWS), 1) // ROWS
    )
    for k in range(CAMS):
        turned = lax.dot_general(
            eye16, rr[k].astype(BF16), (((1,), (1,)), ((), ())), preferred_element_type=F32
        )
        picked = jnp.where(own_row, jnp.concatenate([turned] * ROWS, axis=0), 0.0)
        lbuf[pl.ds(k * NS * ROWS, NS * ROWS)] = jnp.dot(
            picked.astype(BF16), lrow[k], preferred_element_type=F32
        )
    chan_row = lax.broadcasted_iota(jnp.int32, (C, RC), 0)
    chan_lane = lax.rem(lax.broadcasted_iota(jnp.int32, (C, RC), 1), C)
    chan_same = (chan_row == chan_lane).astype(F32)

    def build_rt(i, carry):
        at = (i // NS) * (NS * ROWS) + lax.rem(i, NS)
        for r in range(ROWS):
            row = lbuf[pl.ds(at + r * NS, 1)]
            rt[i, r * C : (r + 1) * C] = (jnp.broadcast_to(row, (C, RC)) * chan_same).astype(BF16)
        return carry

    lax.fori_loop(0, CAMS * NS, build_rt, 0)

    ld_taps.wait()
    ld_width.wait()
    ld_off.wait()
    ld_slane.wait()
    lanes = NS * NW
    width_l = jnp.dot(width[...].astype(F32).astype(BF16), slane[...], preferred_element_type=F32)
    off_l = jnp.dot(off[...].astype(F32).astype(BF16), slane[...], preferred_element_type=F32)
    tap_index = lax.broadcasted_iota(jnp.int32, (TAPS, lanes), 0).astype(F32)
    u_lane = lax.rem(lax.broadcasted_iota(jnp.int32, (1, lanes), 1), NW).astype(F32)
    w_row = lax.broadcasted_iota(jnp.int32, (16, lanes), 0).astype(F32)
    for k in range(CAMS):
        taps_l = jnp.dot(taps[k].astype(BF16), slane[...], preferred_element_type=F32)
        taps_l = jnp.where(tap_index < width_l[k : k + 1], taps_l, 0.0)
        start = u_lane + 32.0 - off_l[k : k + 1]

        def build_band(block, carry):
            gap = start - (w_row + (block * 16).astype(F32))
            value = jnp.zeros((16, lanes), F32)
            for j in range(TAPS):
                value = jnp.where(gap == float(j), taps_l[j : j + 1], value)
            band[k, pl.ds(pl.multiple_of(block * 16, 16), 16)] = value.astype(BF16)
            return carry

        lax.fori_loop(0, 8, build_band, 0)

    ld_exp.wait()
    for copy in sides:
        copy.wait_recv()

    @pl.when(d < ND - 1)
    def _():
        for copy in to_dn:
            copy.wait_recv()

    @pl.when(d > 0)
    def _():
        for copy in to_up:
            copy.wait_recv()

    edges[...] = jnp.dot(expm[...], hc[...], preferred_element_type=F32)
    row16 = lax.broadcasted_iota(jnp.int32, (16, RC), 0)
    first = row16 == 0
    last = row16 == 15

    def build_s1(e, carry):
        x = g2x[e].astype(F32)
        near = edges[pl.ds(pl.multiple_of(e * 16, 16), 16)]
        far = edges[pl.ds(pl.multiple_of((20 + e) * 16, 16), 16)]
        ahead = pltpu.roll(x, NW - 1, 0)
        behind = pltpu.roll(x, 1, 0)
        s1[e, 0:48, 0:RC] = ahead[0:48].astype(BF16)
        s1[e, 48:64, 0:RC] = jnp.where(last, near, ahead[48:64]).astype(BF16)
        s1[e, 64:80, 0:RC] = jnp.where(first, x[0:16], far).astype(BF16)
        s1[e, 0:64, RC : 2 * RC] = g2x[e]
        s1[e, 64:80, RC : 2 * RC] = near.astype(BF16)
        s1[e, 0:16, 2 * RC :] = jnp.where(first, near, behind[0:16]).astype(BF16)
        s1[e, 16:64, 2 * RC :] = behind[16:64].astype(BF16)
        s1[e, 64:80, 2 * RC :] = jnp.where(last, x[48:64], far).astype(BF16)
        return carry

    lax.fori_loop(0, 20, build_s1, 0)

    def conv1(chunk, carry):
        base = chunk * CH1
        total = jnp.zeros((CH1 * 80, RC), F32)
        for td in range(3):
            total = total + jnp.dot(
                s1[pl.ds(base + 2 - td, CH1)].reshape(CH1 * 80, 3 * RC),
                w2[3 * td : 3 * td + 3].reshape(3 * RC, RC),
                preferred_element_type=F32,
            )
        for n in range(CH1):
            f = base + n
            x = jnp.where(pfx[f].astype(F32) > 0, total[n * 80 : n * 80 + 64], 0.0)
            gate = edges[pl.ds(pl.multiple_of((40 + f) * 16, 16), 16)]
            side = jnp.where(gate > 0, total[n * 80 + 64 : n * 80 + 80], 0.0)
            ahead = pltpu.roll(x, NW - 1, 0)
            behind = pltpu.roll(x, 1, 0)
            s2[f, 0:48, 0:RC] = ahead[0:48].astype(BF16)
            s2[f, 48:64, 0:RC] = jnp.where(last, side, ahead[48:64]).astype(BF16)
            s2[f, :, RC : 2 * RC] = x.astype(BF16)
            s2[f, 0:16, 2 * RC :] = jnp.where(first, side, behind[0:16]).astype(BF16)
            s2[f, 16:64, 2 * RC :] = behind[16:64].astype(BF16)
        return carry

    lax.fori_loop(0, 18 // CH1, conv1, 0)

    def conv2(chunk, carry):
        base = chunk * CH2
        total = jnp.zeros((CH2 * NW, RC), F32)
        for td in range(3):
            total = total + jnp.dot(
                s2[pl.ds(base + 2 - td, CH2)].reshape(CH2 * NW, 3 * RC),
                w1[3 * td : 3 * td + 3].reshape(3 * RC, RC),
                preferred_element_type=F32,
            )
        vol[pl.ds(base, CH2)] = total.astype(BF16).reshape(CH2, NW, RC)
        return carry

    lax.fori_loop(0, NS // CH2, conv2, 0)

    def mix(s, carry):
        v = vol[s]
        for k in range(CAMS):
            ymix[k, s] = jnp.dot(v, rt[k * NS + s], preferred_element_type=F32).astype(BF16)
        return carry

    lax.fori_loop(0, NS, mix, 0)

    cams = [
        jnp.dot(band[k], ymix[k].reshape(NS * NW, RC), preferred_element_type=F32)
        for k in range(CAMS)
    ]
    block = lax.broadcasted_iota(jnp.int32, (128, 128), 1) // C
    for r2 in range(ROWS):
        half, turn = r2 // 4, r2 % 4
        parts = [cams[(b - turn) % 4][:, half * 128 : half * 128 + 128] for b in range(4)]
        z = jnp.where(
            block < 2,
            jnp.where(block == 0, parts[0], parts[1]),
            jnp.where(block == 2, parts[2], parts[3]),
        )
        zbuf[r2] = z.astype(BF16)

    def back(i, j, src_row, rows, dst_row, col):
        t = lax.rem(d + j, ND)
        return pltpu.make_async_remote_copy(
            src_ref=zbuf.at[t, pl.ds(src_row, rows)],
            dst_ref=rbuf.at[j, pl.ds(dst_row, rows)],
            send_sem=bs_sem.at[i, j], recv_sem=br_sem.at[i, j],
            device_id={"depth": t, "azim": col}, device_id_type=pl.DeviceIdType.MESH,
        )

    copies = []
    for j in list(range(1, ND)) + [0]:
        if j:
            copies.append(back(0, j, 32, 64, 0, a))
        copies.append(back(1, j, 96, 32, 64, a_up))
        copies.append(back(2, j, 0, 32, 96, a_dn))
    for copy in copies:
        copy.start()
    rbuf[0, 0:64] = zbuf[d, 32:96]

    for copy in copies:
        copy.wait_recv()
    total = jnp.zeros((NW, 128), F32)
    for j in range(ND):
        total = total + (rbuf[j, 0:64].astype(F32) + rbuf[j, 64:128].astype(F32))
    turn = lax.rem(d, 4)
    out_ref[0] = pltpu.roll(total, lax.rem(4 - turn, 4) * C, 1)

    for copy in copies:
        copy.wait_send()
    for copy in sides:
        copy.wait_send()

    @pl.when(d < ND - 1)
    def _():
        for copy in to_up:
            copy.wait_send()

    @pl.when(d > 0)
    def _():
        for copy in to_dn:
            copy.wait_send()


def body(cotangent, pre_second, pre_first, kernel_first, kernel_second, row_resample, col_taps, band_width, col_offset):
    consts = [
        jnp.asarray(x, BF16)
        for x in (stage_select(), edge_expand(), row_place(), lane_rows(), sphere_lanes())
    ]
    vm = pltpu.VMEM
    scratch = [
        vm((NS, NW, RC), BF16), vm((NS, NW, RC), BF16), vm((18, NW, RC), BF16),
        vm((20, NW, RC), BF16), vm((2, 9, 96, C), BF16), vm((CAMS, ROWS * ROWS, NS), F32),
        vm((CAMS, TAPS, NS), F32), vm((CAMS, NS), jnp.int32), vm((CAMS, NS), jnp.int32),
        vm((160, 1024), BF16), vm((58 * 16, 160), BF16), vm((ROWS, 96, RC), BF16),
        vm((CAMS, ROWS * ROWS, RC), BF16), vm((NS, NS * NW), BF16),
        vm((160, RC), BF16), vm((160, RC), BF16),
        vm((20, 80, 3 * RC), BF16), vm((18, NW, 3 * RC), BF16), vm((16, RC), F32),
        vm((58 * 16, RC), F32), vm((2, 288, 96), BF16),
        vm((9, RC, RC), BF16), vm((9, RC, RC), BF16),
        vm((CAMS * NS * ROWS, RC), F32), vm((CAMS * NS, RC, RC), BF16),
        vm((CAMS, 128, NS * NW), BF16), vm((NS, NW, RC), BF16), vm((CAMS, NS, NW, RC), BF16),
        vm((ROWS, 128, 128), BF16), vm((ND, 128, 128), BF16),
        pltpu.SemaphoreType.DMA((14,)), pltpu.SemaphoreType.DMA((10,)),
        pltpu.SemaphoreType.DMA((10,)), pltpu.SemaphoreType.DMA((3, ND)),
        pltpu.SemaphoreType.DMA((3, ND)),
    ]
    return pl.pallas_call(
        kernel,
        out_shape=jax.ShapeDtypeStruct((1, NW, 128), F32),
        in_specs=[pl.BlockSpec(memory_space=pl.ANY)] * 14,
        out_specs=pl.BlockSpec(memory_space=pltpu.VMEM),
        scratch_shapes=scratch,
        compiler_params=pltpu.CompilerParams(
            collective_id=0, has_side_effects=True, vmem_limit_bytes=62 * 1024 * 1024
        ),
    )(
        cotangent, pre_second, pre_first,
        kernel_first.reshape(9, 96, C), kernel_second.reshape(9, 96, C),
        row_resample.transpose(0, 2, 3, 1).reshape(CAMS, ROWS * ROWS, NS), col_taps.transpose(0, 2, 1),
        band_width, col_offset, *consts,
    )


def solution(mesh):
    placed = (
        P("depth", "azim", None),
        P("depth", "azim", None),
        P("depth", "azim", None),
        P(),
        P(),
        P(None, "depth", None, None),
        P(None, "depth", None),
        P(None, "depth"),
        P(None, "depth"),
    )
    return jax.shard_map(
        body, mesh=mesh, in_specs=placed, out_specs=P("depth", "azim", None), check_vma=False
    )
```

time: 189 us -> 36.7 us (0.19)
  the two profiles are of different devices: /device:TPU:4 before, /device:TPU:1 now
where the time goes in v1:
time: 36.7 us; the launch traced here: 36.5 us
  Pallas kernels  35.2 us (96%)
  local copies, waits for them, and re-layouts  1.38 us (4%)
    pallas_call x1, Pallas kernels, body(): pl.pallas_call(kernel, out_shape=jax.ShapeDtypeStruct((1, NW, 128), F32),...  35.2 us
    unnamed x1, local copies, waits for them, and re-layouts  1.38 us

profile of v1, /device:TPU:1, one launch (start us, length us, event | category | flops | bytes accessed | tf_op | source)
XLA Modules:
  0.0 36.5 jit_solution(3463519797406224383)
XLA Ops:
  0.0 35.2 %shard_map.136 = f32[1,64,128]{2,1,0:T(8,128)} custom-call(bf16[16,64,256]{2,1,0:T(8,128)(2,1)} %cot_h.1, bf16[16,64,256]{2,1,0:T(8,128)(2,1)} %pre2_h.1, bf16[16,64,256]{2,1,0:T(8,128)(2,1)} %pre1_h.1, bf16[9,96,32]{2,1,0:T(8,128)(2,1)} %bitcast.6, bf16[9,96,32]{2,1,0:T(8,128)(2,1)} %bitcast.7, f32[4,64,16]{2,1,0:T(8,128)} %bitcast.8, f32[4,8,16]{2,1,0:T(8,128)} %bitcast.9, ...), custom_call_target="tpu_custom_call" | custom-call | tf_op jit(solution)/shard_map/pallas_call | solution.py:441
  35.2 1.4 %copy.16 = f32[1,64,128]{2,1,0:T(8,128)} copy(f32[1,64,128]{2,1,0:T(8,128)} %shard_map.136) | data formatting | bytes 65536

commit v2 on v1

--- a/solution.py
+++ b/solution.py
@@ -68,22 +68,23 @@
 
 
 def row_place():
-    place = np.zeros((ROWS, 3, C, ROWS, C), np.float32)
+    place = np.zeros((2, ROWS, 3, C, RC), np.float32)
+    i = np.arange(C)
     for r_in in range(ROWS):
         for tap in range(3):
             r_out = r_in - 1 + tap
             if 0 <= r_out < ROWS:
-                place[r_in, tap, np.arange(C), r_out, np.arange(C)] = 1
-    return place.reshape(ROWS, 3 * C, RC)
+                place[0, r_in, tap, i, r_out * C + i] = 1
+                place[1, r_in, tap, i, (i // 16) * 128 + r_out * 16 + i % 16] = 1
+    return place.reshape(2, ROWS, 3 * C, RC)
 
 
 def lane_rows():
-    out = np.zeros((CAMS, ROWS, ROWS, RC), np.float32)
-    lane = np.arange(RC)
+    out = np.zeros((CAMS, ROWS, ROWS, 128), np.float32)
+    lane = np.arange(128)
     for k in range(CAMS):
-        row = 4 * (lane // 128) + ((lane % 128) // 32 - k) % 4
-        out[k, :, row, lane] = 1
-    return out.reshape(CAMS, ROWS * ROWS, RC)
+        out[k, :, (lane // 16 - 2 * k) % 8, lane] = 1
+    return out.reshape(CAMS, ROWS * ROWS, 128)
 
 
 def sphere_lanes():
@@ -166,29 +167,29 @@
 
     pl.semaphore_wait(barrier, 3 * ND - 1)
 
-    def remote(i, src, dst, dep, col):
+    def remote(group, src, dst, dep, col):
         return pltpu.make_async_remote_copy(
-            src_ref=src, dst_ref=dst, send_sem=fs_sem.at[i], recv_sem=fr_sem.at[i],
+            src_ref=src, dst_ref=dst, send_sem=fs_sem.at[group], recv_sem=fr_sem.at[group],
             device_id={"depth": dep, "azim": col}, device_id_type=pl.DeviceIdType.MESH,
         )
 
     up = jnp.minimum(d + 1, ND - 1)
     dn = jnp.maximum(d - 1, 0)
     to_up = [
-        remote(0, g2x.at[pl.ds(16, 2)], g2x.at[pl.ds(0, 2)], up, a),
+        remote(1, g2x.at[pl.ds(16, 2)], g2x.at[pl.ds(0, 2)], up, a),
         remote(1, pfx.at[pl.ds(16, 1)], pfx.at[pl.ds(0, 1)], up, a),
-        remote(2, stage.at[pl.ds(96, 16)], hc.at[pl.ds(96, 16)], up, a_up),
-        remote(3, stage.at[pl.ds(112, 16)], hc.at[pl.ds(112, 16)], up, a_dn),
+        remote(1, stage.at[pl.ds(96, 16)], hc.at[pl.ds(96, 16)], up, a_up),
+        remote(1, stage.at[pl.ds(112, 16)], hc.at[pl.ds(112, 16)], up, a_dn),
     ]
     to_dn = [
-        remote(4, g2x.at[pl.ds(2, 2)], g2x.at[pl.ds(18, 2)], dn, a),
-        remote(5, pfx.at[pl.ds(1, 1)], pfx.at[pl.ds(17, 1)], dn, a),
-        remote(6, stage.at[pl.ds(128, 16)], hc.at[pl.ds(128, 16)], dn, a_up),
-        remote(7, stage.at[pl.ds(144, 16)], hc.at[pl.ds(144, 16)], dn, a_dn),
+        remote(2, g2x.at[pl.ds(2, 2)], g2x.at[pl.ds(18, 2)], dn, a),
+        remote(2, pfx.at[pl.ds(1, 1)], pfx.at[pl.ds(17, 1)], dn, a),
+        remote(2, stage.at[pl.ds(128, 16)], hc.at[pl.ds(128, 16)], dn, a_up),
+        remote(2, stage.at[pl.ds(144, 16)], hc.at[pl.ds(144, 16)], dn, a_dn),
     ]
     sides = [
-        remote(8, stage.at[pl.ds(0, 48)], hc.at[pl.ds(0, 48)], d, a_up),
-        remote(9, stage.at[pl.ds(48, 48)], hc.at[pl.ds(48, 48)], d, a_dn),
+        remote(0, stage.at[pl.ds(0, 48)], hc.at[pl.ds(0, 48)], d, a_up),
+        remote(0, stage.at[pl.ds(48, 48)], hc.at[pl.ds(48, 48)], d, a_dn),
     ]
     for copy in sides:
         copy.start()
@@ -202,6 +203,10 @@
     def _():
         for copy in to_dn:
             copy.start()
+
+    def drain(sem, rows):
+        view = w2.at[0, pl.ds(0, rows)]
+        pltpu.make_async_copy(view, view, sem).wait()
 
     ld_k2.wait()
     ld_k1.wait()
@@ -215,7 +220,7 @@
                 eye, kk[layer, pair], (((1,), (1,)), ((), ())), preferred_element_type=F32
             ).astype(BF16)
         for r_in in range(ROWS):
-            mixed = jnp.dot(kc[layer], place[r_in], preferred_element_type=F32)
+            mixed = jnp.dot(kc[layer], place[layer, r_in], preferred_element_type=F32)
             w[:, pl.ds(r_in * C, C), :] = mixed.astype(BF16).reshape(9, C, RC)
 
     ld_rr.wait()
@@ -235,18 +240,20 @@
         lbuf[pl.ds(k * NS * ROWS, NS * ROWS)] = jnp.dot(
             picked.astype(BF16), lrow[k], preferred_element_type=F32
         )
-    chan_row = lax.broadcasted_iota(jnp.int32, (C, RC), 0)
-    chan_lane = lax.rem(lax.broadcasted_iota(jnp.int32, (C, RC), 1), C)
+    chan_row = lax.broadcasted_iota(jnp.int32, (16, 128), 0)
+    chan_lane = lax.rem(lax.broadcasted_iota(jnp.int32, (16, 128), 1), 16)
     chan_same = (chan_row == chan_lane).astype(F32)
 
-    def build_rt(i, carry):
-        at = (i // NS) * (NS * ROWS) + lax.rem(i, NS)
-        for r in range(ROWS):
-            row = lbuf[pl.ds(at + r * NS, 1)]
-            rt[i, r * C : (r + 1) * C] = (jnp.broadcast_to(row, (C, RC)) * chan_same).astype(BF16)
+    def build_rt(s, carry):
+        for k in range(CAMS):
+            for r in range(ROWS):
+                row = lbuf[pl.ds((k * ROWS + r) * NS + s, 1)]
+                rt[s, r * 16 : (r + 1) * 16, k * 128 : (k + 1) * 128] = (
+                    jnp.broadcast_to(row, (16, 128)) * chan_same
+                ).astype(BF16)
         return carry
 
-    lax.fori_loop(0, CAMS * NS, build_rt, 0)
+    lax.fori_loop(0, NS, build_rt, 0)
 
     ld_taps.wait()
     ld_width.wait()
@@ -257,35 +264,35 @@
     off_l = jnp.dot(off[...].astype(F32).astype(BF16), slane[...], preferred_element_type=F32)
     tap_index = lax.broadcasted_iota(jnp.int32, (TAPS, lanes), 0).astype(F32)
     u_lane = lax.rem(lax.broadcasted_iota(jnp.int32, (1, lanes), 1), NW).astype(F32)
-    w_row = lax.broadcasted_iota(jnp.int32, (16, lanes), 0).astype(F32)
+    w_row = lax.broadcasted_iota(jnp.int32, (16, lanes), 0).astype(F32).astype(BF16)
     for k in range(CAMS):
         taps_l = jnp.dot(taps[k].astype(BF16), slane[...], preferred_element_type=F32)
         taps_l = jnp.where(tap_index < width_l[k : k + 1], taps_l, 0.0)
-        start = u_lane + 32.0 - off_l[k : k + 1]
+        wide = [
+            jnp.broadcast_to(taps_l[j : j + 1], (16, lanes)).astype(BF16) for j in range(TAPS)
+        ]
+        start = jnp.broadcast_to(u_lane + 32.0 - off_l[k : k + 1], (16, lanes)).astype(BF16) - w_row
 
         def build_band(block, carry):
-            gap = start - (w_row + (block * 16).astype(F32))
-            value = jnp.zeros((16, lanes), F32)
+            gap = start - (block * 16).astype(F32).astype(BF16)
+            value = jnp.zeros((16, lanes), BF16)
             for j in range(TAPS):
-                value = jnp.where(gap == float(j), taps_l[j : j + 1], value)
-            band[k, pl.ds(pl.multiple_of(block * 16, 16), 16)] = value.astype(BF16)
+                value = jnp.where(gap == jnp.asarray(j, BF16), wide[j], value)
+            band[k, pl.ds(pl.multiple_of(block * 16, 16), 16)] = value
             return carry
 
         lax.fori_loop(0, 8, build_band, 0)
 
     ld_exp.wait()
-    for copy in sides:
-        copy.wait_recv()
+    drain(fr_sem.at[0], 96)
 
     @pl.when(d < ND - 1)
     def _():
-        for copy in to_dn:
-            copy.wait_recv()
+        drain(fr_sem.at[2], 224)
 
     @pl.when(d > 0)
     def _():
-        for copy in to_up:
-            copy.wait_recv()
+        drain(fr_sem.at[1], 224)
 
     edges[...] = jnp.dot(expm[...], hc[...], preferred_element_type=F32)
     row16 = lax.broadcasted_iota(jnp.int32, (16, RC), 0)
@@ -347,72 +354,64 @@
         vol[pl.ds(base, CH2)] = total.astype(BF16).reshape(CH2, NW, RC)
         return carry
 
-    lax.fori_loop(0, NS // CH2, conv2, 0)
+    lax.fori_loop(0, NS // CH2, conv2, 0, unroll=True)
 
     def mix(s, carry):
-        v = vol[s]
+        v = jnp.concatenate([vol[s, :, 0:128], vol[s, :, 128:256]], axis=0)
+        y = jnp.dot(v, rt[s], preferred_element_type=F32).astype(BF16)
         for k in range(CAMS):
-            ymix[k, s] = jnp.dot(v, rt[k * NS + s], preferred_element_type=F32).astype(BF16)
+            ymix[k, s, :, 0:128] = y[0:64, k * 128 : k * 128 + 128]
+            ymix[k, s, :, 128:256] = y[64:128, k * 128 : k * 128 + 128]
         return carry
 
-    lax.fori_loop(0, NS, mix, 0)
-
-    cams = [
-        jnp.dot(band[k], ymix[k].reshape(NS * NW, RC), preferred_element_type=F32)
-        for k in range(CAMS)
-    ]
-    block = lax.broadcasted_iota(jnp.int32, (128, 128), 1) // C
+    lax.fori_loop(0, NS, mix, 0, unroll=True)
+
+    source = []
+    for k in range(CAMS):
+        cam = jnp.dot(band[k], ymix[k].reshape(NS * NW, RC), preferred_element_type=F32)
+        source.append(cam[:, 0:128].astype(BF16))
+        source.append(pltpu.roll(cam[:, 128:256], 16, 1).astype(BF16))
+    block = lax.broadcasted_iota(jnp.int32, (128, 128), 1) // 16
     for r2 in range(ROWS):
-        half, turn = r2 // 4, r2 % 4
-        parts = [cams[(b - turn) % 4][:, half * 128 : half * 128 + 128] for b in range(4)]
-        z = jnp.where(
-            block < 2,
-            jnp.where(block == 0, parts[0], parts[1]),
-            jnp.where(block == 2, parts[2], parts[3]),
-        )
-        zbuf[r2] = z.astype(BF16)
-
-    def back(i, j, src_row, rows, dst_row, col):
+        z = source[0]
+        for q in range(1, ROWS):
+            z = jnp.where(block == (r2 + q) % 8, source[q], z)
+        zbuf[r2] = z
+
+    def back(j, src_row, rows, dst_row, col):
         t = lax.rem(d + j, ND)
         return pltpu.make_async_remote_copy(
             src_ref=zbuf.at[t, pl.ds(src_row, rows)],
-            dst_ref=rbuf.at[j, pl.ds(dst_row, rows)],
-            send_sem=bs_sem.at[i, j], recv_sem=br_sem.at[i, j],
+            dst_ref=rbuf.at[pl.ds(j * 128 + dst_row, rows)],
+            send_sem=bs_sem, recv_sem=br_sem,
             device_id={"depth": t, "azim": col}, device_id_type=pl.DeviceIdType.MESH,
         )
 
-    copies = []
     for j in list(range(1, ND)) + [0]:
         if j:
-            copies.append(back(0, j, 32, 64, 0, a))
-        copies.append(back(1, j, 96, 32, 64, a_up))
-        copies.append(back(2, j, 0, 32, 96, a_dn))
-    for copy in copies:
-        copy.start()
-    rbuf[0, 0:64] = zbuf[d, 32:96]
-
-    for copy in copies:
-        copy.wait_recv()
+            back(j, 32, 64, 0, a).start()
+        back(j, 96, 32, 64, a_up).start()
+        back(j, 0, 32, 96, a_dn).start()
+    rbuf[0:64] = zbuf[d, 32:96]
+
+    arrived = rbuf.at[pl.ds(64, ND * 128 - 64)]
+    pltpu.make_async_copy(arrived, arrived, br_sem).wait()
     total = jnp.zeros((NW, 128), F32)
     for j in range(ND):
-        total = total + (rbuf[j, 0:64].astype(F32) + rbuf[j, 64:128].astype(F32))
-    turn = lax.rem(d, 4)
-    out_ref[0] = pltpu.roll(total, lax.rem(4 - turn, 4) * C, 1)
-
-    for copy in copies:
-        copy.wait_send()
-    for copy in sides:
-        copy.wait_send()
+        own = rbuf[j * 128 : j * 128 + 64].astype(F32)
+        total = total + (own + rbuf[j * 128 + 64 : j * 128 + 128].astype(F32))
+    out_ref[0] = pltpu.roll(total, lax.rem(ND - d, ND) * 16, 1)
+
+    pltpu.make_async_copy(arrived, arrived, bs_sem).wait()
+    drain(fs_sem.at[0], 96)
 
     @pl.when(d < ND - 1)
     def _():
-        for copy in to_up:
-            copy.wait_send()
+        drain(fs_sem.at[1], 224)
 
     @pl.when(d > 0)
     def _():
-        for copy in to_dn:
-            copy.wait_send()
+        drain(fs_sem.at[2], 224)
 
 
 def body(cotangent, pre_second, pre_first, kernel_first, kernel_second, row_resample, col_taps, band_width, col_offset):
@@ -425,18 +424,17 @@
         vm((NS, NW, RC), BF16), vm((NS, NW, RC), BF16), vm((18, NW, RC), BF16),
         vm((20, NW, RC), BF16), vm((2, 9, 96, C), BF16), vm((CAMS, ROWS * ROWS, NS), F32),
         vm((CAMS, TAPS, NS), F32), vm((CAMS, NS), jnp.int32), vm((CAMS, NS), jnp.int32),
-        vm((160, 1024), BF16), vm((58 * 16, 160), BF16), vm((ROWS, 96, RC), BF16),
-        vm((CAMS, ROWS * ROWS, RC), BF16), vm((NS, NS * NW), BF16),
+        vm((160, 1024), BF16), vm((58 * 16, 160), BF16), vm((2, ROWS, 96, RC), BF16),
+        vm((CAMS, ROWS * ROWS, 128), BF16), vm((NS, NS * NW), BF16),
         vm((160, RC), BF16), vm((160, RC), BF16),
         vm((20, 80, 3 * RC), BF16), vm((18, NW, 3 * RC), BF16), vm((16, RC), F32),
         vm((58 * 16, RC), F32), vm((2, 288, 96), BF16),
         vm((9, RC, RC), BF16), vm((9, RC, RC), BF16),
-        vm((CAMS * NS * ROWS, RC), F32), vm((CAMS * NS, RC, RC), BF16),
+        vm((CAMS * NS * ROWS, 128), F32), vm((NS, 128, CAMS * 128), BF16),
         vm((CAMS, 128, NS * NW), BF16), vm((NS, NW, RC), BF16), vm((CAMS, NS, NW, RC), BF16),
-        vm((ROWS, 128, 128), BF16), vm((ND, 128, 128), BF16),
-        pltpu.SemaphoreType.DMA((14,)), pltpu.SemaphoreType.DMA((10,)),
-        pltpu.SemaphoreType.DMA((10,)), pltpu.SemaphoreType.DMA((3, ND)),
-        pltpu.SemaphoreType.DMA((3, ND)),
+        vm((ROWS, 128, 128), BF16), vm((ND * 128, 128), BF16),
+        pltpu.SemaphoreType.DMA((14,)), pltpu.SemaphoreType.DMA((3,)),
+        pltpu.SemaphoreType.DMA((3,)), pltpu.SemaphoreType.DMA, pltpu.SemaphoreType.DMA,
     ]
     return pl.pallas_call(
         kernel,

time: 36.7 us -> 32.1 us (0.87)
  Pallas kernels: 35.2 us -> 30.4 us
    pallas_call x1, Pallas kernels: 35.2 us -> 30.4 us  [body(): pl.pallas_call(kernel, out_shape=jax.ShapeDtypeStruct((1, NW, 128), F32),...]
where the time goes in v2:
time: 32.1 us; the launch traced here: 31.8 us
  Pallas kernels  30.4 us (95%)
  local copies, waits for them, and re-layouts  1.38 us (4%)
    pallas_call x1, Pallas kernels, body(): pl.pallas_call(kernel, out_shape=jax.ShapeDtypeStruct((1, NW, 128), F32),...  30.4 us
    unnamed x1, local copies, waits for them, and re-layouts  1.38 us

profile of v2, /device:TPU:1, one launch (start us, length us, event | category | flops | bytes accessed | tf_op | source)
XLA Modules:
  0.0 31.8 jit_solution(4879201049544358048)
XLA Ops:
  0.0 30.4 %shard_map.136 = f32[1,64,128]{2,1,0:T(8,128)} custom-call(bf16[16,64,256]{2,1,0:T(8,128)(2,1)} %cot_h.1, bf16[16,64,256]{2,1,0:T(8,128)(2,1)} %pre2_h.1, bf16[16,64,256]{2,1,0:T(8,128)(2,1)} %pre1_h.1, bf16[9,96,32]{2,1,0:T(8,128)(2,1)} %bitcast.6, bf16[9,96,32]{2,1,0:T(8,128)(2,1)} %bitcast.7, f32[4,64,16]{2,1,0:T(8,128)} %bitcast.8, f32[4,8,16]{2,1,0:T(8,128)} %bitcast.9, ...), custom_call_target="tpu_custom_call" | custom-call | tf_op jit(solution)/shard_map/pallas_call | solution.py:439
  30.4 1.4 %copy.16 = f32[1,64,128]{2,1,0:T(8,128)} copy(f32[1,64,128]{2,1,0:T(8,128)} %shard_map.136) | data formatting | bytes 65536

commit v3 on v2

v3 whole, which is shorter than its diff:
```python
import numpy as np
import jax
import jax.numpy as jnp
from jax import lax
from jax.experimental import pallas as pl
from jax.experimental.pallas import tpu as pltpu
from jax.sharding import PartitionSpec as P

TAPS = 8
SHIFT = 24
NS = 16
NW = 64
ROWS = 8
C = 32
RC = ROWS * C
CAMS = 4
ND = 8
F32 = jnp.float32
BF16 = jnp.bfloat16
EARLYB = 1
EARLYR = 0
EARLYW = 0
US2 = 3
CH1 = 7
CH2 = 8


def stage_select():
    sel = np.zeros((160, 1024), np.float32)

    def at(array, sphere, column):
        part = 2 * array + (0 if column < 16 else 1)
        return 256 * part + 16 * sphere + column % 16

    for s in range(NS):
        sel[s, at(0, s, 62)] = 1
        sel[16 + s, at(0, s, 63)] = 1
        sel[32 + s, at(1, s, 63)] = 1
        sel[48 + s, at(0, s, 0)] = 1
        sel[64 + s, at(0, s, 1)] = 1
        sel[80 + s, at(1, s, 0)] = 1
    corners = ((96, 14, 62), (112, 14, 0), (128, 0, 62), (144, 0, 0))
    for base, sphere, column in corners:
        for i in range(4):
            sel[base + i, at(0, sphere + i // 2, column + i % 2)] = 1
        pf_sphere = 15 if sphere == 14 else 0
        pf_column = 63 if column == 62 else 0
        sel[base + 4, at(1, pf_sphere, pf_column)] = 1
    return sel


def edge_expand():
    mat = np.zeros((3 * 20 + 18, 16, 160), np.float32)
    for e in range(20):
        if e < 2:
            left, right = [96 + 2 * e, 97 + 2 * e], [112 + 2 * e, 113 + 2 * e]
        elif e < 18:
            left, right = [e - 2, 16 + e - 2], [48 + e - 2, 64 + e - 2]
        else:
            f = e - 18
            left, right = [128 + 2 * f, 129 + 2 * f], [144 + 2 * f, 145 + 2 * f]
        mat[e, 14, right[1]] = 1
        mat[e, 15, right[0]] = 1
        mat[20 + e, 1, left[1]] = 1
        mat[20 + e, 14, right[0]] = 1
        mat[40 + e, 0, left[1]] = 1
        mat[40 + e, 1, left[0]] = 1
    for f in range(18):
        left = 100 if f == 0 else 132 if f == 17 else 32 + f - 1
        right = 116 if f == 0 else 148 if f == 17 else 80 + f - 1
        mat[60 + f, 1, left] = 1
        mat[60 + f, 14, right] = 1
    return mat.reshape(-1, 160)


def row_place():
    place = np.zeros((2, ROWS, 3, C, RC), np.float32)
    i = np.arange(C)
    for r_in in range(ROWS):
        for tap in range(3):
            r_out = r_in - 1 + tap
            if 0 <= r_out < ROWS:
                place[0, r_in, tap, i, r_out * C + i] = 1
                place[1, r_in, tap, i, (i // 16) * 128 + r_out * 16 + i % 16] = 1
    return place.reshape(2, ROWS, 3 * C, RC)


def lane_rows():
    out = np.zeros((CAMS, ROWS, ROWS, 128), np.float32)
    lane = np.arange(128)
    for k in range(CAMS):
        out[k, :, (lane // 16 - 2 * k) % 8, lane] = 1
    return out.reshape(CAMS, ROWS * ROWS, 128)


def sphere_lanes():
    out = np.zeros((NS, NS * NW), np.float32)
    out[np.arange(NS * NW) // NW, np.arange(NS * NW)] = 1
    return out


def kernel(
    cot_h, pre2_h, pre1_h, k1_h, k2_h, rr_h, taps_h, width_h, off_h,
    sel_h, exp_h, place_h, lrow_h, slane_h,
    out_ref,
    cot, pre2, pfx, g2x, kk, rr, taps, width, off,
    sel, expm, place, lrow, slane,
    stage, hc, s1, t1, s2, hidden, fix, edges, kc, w2, w1, lbuf, rt, band, vol, ymix, zbuf, rbuf,
    in_sem, fs_sem, fr_sem, bs_sem, br_sem,
):
    d = lax.axis_index("depth")
    a = lax.axis_index("azim")
    na = lax.axis_size("azim")
    a_up = lax.rem(a + 1, na)
    a_dn = lax.rem(a + na - 1, na)

    def load(i, src, dst):
        copy = pltpu.make_async_copy(src, dst, in_sem.at[i])
        copy.start()
        return copy

    ld_cot = load(0, cot_h, cot)
    ld_pre2 = load(1, pre2_h, pre2)
    ld_taps = load(9, taps_h, taps)
    ld_width = load(10, width_h, width)
    ld_off = load(11, off_h, off)
    ld_slane = load(12, slane_h, slane)
    ld_pre1 = load(2, pre1_h, pfx.at[pl.ds(1, NS)])
    ld_sel = load(3, sel_h, sel)

    barrier = pltpu.get_barrier_semaphore()
    for j in range(ND):
        t = lax.rem(d + j, ND)
        for col in (a_dn, a, a_up):
            if j == 0 and col is a:
                continue
            pl.semaphore_signal(
                barrier, inc=1, device_id={"depth": t, "azim": col},
                device_id_type=pl.DeviceIdType.MESH,
            )

    ld_rr = load(7, rr_h, rr)
    ld_lrow = load(8, lrow_h, lrow)
    ld_k2 = load(4, k2_h, kk.at[0])
    ld_place = load(6, place_h, place)
    ld_k1 = load(5, k1_h, kk.at[1])
    ld_exp = load(13, exp_h, expm)

    @pl.when(d == 0)
    def _():
        g2x[0:2] = jnp.zeros((2, NW, RC), BF16)
        pfx[0:1] = jnp.zeros((1, NW, RC), BF16)
        hc[96:128] = jnp.zeros((32, RC), BF16)

    @pl.when(d == ND - 1)
    def _():
        g2x[18:20] = jnp.zeros((2, NW, RC), BF16)
        pfx[17:18] = jnp.zeros((1, NW, RC), BF16)
        hc[128:160] = jnp.zeros((32, RC), BF16)

    def build_mixers():
        ld_k2.wait()
        ld_k1.wait()
        ld_place.wait()
        eye = (
            lax.broadcasted_iota(jnp.int32, (C, C), 0) == lax.broadcasted_iota(jnp.int32, (C, C), 1)
        ).astype(BF16)
        for layer, w in enumerate((w2, w1)):
            for pair in range(9):
                kc[layer, pl.ds(pair * C, C)] = lax.dot_general(
                    eye, kk[layer, pair], (((1,), (1,)), ((), ())), preferred_element_type=F32
                ).astype(BF16)
            for r_in in range(ROWS):
                mixed = jnp.dot(kc[layer], place[layer, r_in], preferred_element_type=F32)
                w[:, pl.ds(r_in * C, C), :] = mixed.astype(BF16).reshape(9, C, RC)

    def build_resample():
        ld_rr.wait()
        ld_lrow.wait()
        eye16 = (
            lax.broadcasted_iota(jnp.int32, (NS, NS), 0) == lax.broadcasted_iota(jnp.int32, (NS, NS), 1)
        ).astype(BF16)
        own_row = (
            lax.broadcasted_iota(jnp.int32, (ROWS * NS, ROWS * ROWS), 0) // NS
            == lax.broadcasted_iota(jnp.int32, (ROWS * NS, ROWS * ROWS), 1) // ROWS
        )
        for k in range(CAMS):
            turned = lax.dot_general(
                eye16, rr[k].astype(BF16), (((1,), (1,)), ((), ())), preferred_element_type=F32
            )
            picked = jnp.where(own_row, jnp.concatenate([turned] * ROWS, axis=0), 0.0)
            lbuf[pl.ds(k * NS * ROWS, NS * ROWS)] = jnp.dot(
                picked.astype(BF16), lrow[k], preferred_element_type=F32
            )
        chan_row = lax.broadcasted_iota(jnp.int32, (16, 128), 0)
        chan_lane = lax.rem(lax.broadcasted_iota(jnp.int32, (16, 128), 1), 16)
        chan_same = (chan_row == chan_lane).astype(F32)

        def build_rt(s, carry):
            for k in range(CAMS):
                for r in range(ROWS):
                    row = lbuf[pl.ds((k * ROWS + r) * NS + s, 1)]
                    rt[s, r * 16 : (r + 1) * 16, k * 128 : (k + 1) * 128] = (
                        jnp.broadcast_to(row, (16, 128)) * chan_same
                    ).astype(BF16)
            return carry

        lax.fori_loop(0, NS, build_rt, 0)

    def build_bands():
        ld_taps.wait()
        ld_width.wait()
        ld_off.wait()
        ld_slane.wait()
        lanes = NS * NW
        width_l = jnp.dot(width[...].astype(F32).astype(BF16), slane[...], preferred_element_type=F32)
        off_l = jnp.dot(off[...].astype(F32).astype(BF16), slane[...], preferred_element_type=F32)
        tap_index = lax.broadcasted_iota(jnp.int32, (TAPS, lanes), 0).astype(F32)
        u_lane = lax.rem(lax.broadcasted_iota(jnp.int32, (1, lanes), 1), NW).astype(F32)
        w_row = lax.broadcasted_iota(jnp.int32, (16, lanes), 0).astype(F32).astype(BF16)
        for k in range(CAMS):
            taps_l = jnp.dot(taps[k].astype(BF16), slane[...], preferred_element_type=F32)
            taps_l = jnp.where(tap_index < width_l[k : k + 1], taps_l, 0.0)
            wide = [
                jnp.broadcast_to(taps_l[j : j + 1], (16, lanes)).astype(BF16) for j in range(TAPS)
            ]
            start = jnp.broadcast_to(u_lane + 32.0 - off_l[k : k + 1], (16, lanes)).astype(BF16) - w_row

            def build_band(block, carry):
                gap = start - lax.rem(block * 16 + 96, 128).astype(F32).astype(BF16)
                value = jnp.zeros((16, lanes), BF16)
                for j in range(TAPS):
                    value = jnp.where(gap == jnp.asarray(j, BF16), wide[j], value)
                band[k, pl.ds(pl.multiple_of(block * 16, 16), 16)] = value
                return carry

            lax.fori_loop(0, 8, build_band, 0)

    if EARLYB:
        build_bands()
    if EARLYR:
        build_resample()
    if EARLYW:
        build_mixers()
    ld_cot.wait()
    ld_pre2.wait()
    g2x[2:18] = jnp.where(pre2[...] > 0, cot[...], jnp.zeros((), BF16))
    ld_pre1.wait()
    ld_sel.wait()
    acc = jnp.zeros((160, RC), F32)
    for part, ref in enumerate((g2x.at[2:18, 0:16], g2x.at[2:18, 48:64],
                                pfx.at[1:17, 0:16], pfx.at[1:17, 48:64])):
        acc = acc + jnp.dot(
            sel[:, 256 * part : 256 * part + 256], ref[...].reshape(256, RC),
            preferred_element_type=F32,
        )
    stage[...] = acc.astype(BF16)

    pl.semaphore_wait(barrier, 3 * ND - 1)

    def remote(group, src, dst, dep, col):
        return pltpu.make_async_remote_copy(
            src_ref=src, dst_ref=dst, send_sem=fs_sem.at[group], recv_sem=fr_sem.at[group],
            device_id={"depth": dep, "azim": col}, device_id_type=pl.DeviceIdType.MESH,
        )

    up = jnp.minimum(d + 1, ND - 1)
    dn = jnp.maximum(d - 1, 0)
    to_up = [
        remote(1, g2x.at[pl.ds(16, 2)], g2x.at[pl.ds(0, 2)], up, a),
        remote(1, pfx.at[pl.ds(16, 1)], pfx.at[pl.ds(0, 1)], up, a),
        remote(1, stage.at[pl.ds(96, 16)], hc.at[pl.ds(96, 16)], up, a_up),
        remote(1, stage.at[pl.ds(112, 16)], hc.at[pl.ds(112, 16)], up, a_dn),
    ]
    to_dn = [
        remote(2, g2x.at[pl.ds(2, 2)], g2x.at[pl.ds(18, 2)], dn, a),
        remote(2, pfx.at[pl.ds(1, 1)], pfx.at[pl.ds(17, 1)], dn, a),
        remote(2, stage.at[pl.ds(128, 16)], hc.at[pl.ds(128, 16)], dn, a_up),
        remote(2, stage.at[pl.ds(144, 16)], hc.at[pl.ds(144, 16)], dn, a_dn),
    ]
    sides = [
        remote(0, stage.at[pl.ds(0, 48)], hc.at[pl.ds(0, 48)], d, a_up),
        remote(0, stage.at[pl.ds(48, 48)], hc.at[pl.ds(48, 48)], d, a_dn),
    ]
    for copy in sides:
        copy.start()

    @pl.when(d < ND - 1)
    def _():
        for copy in to_up:
            copy.start()

    @pl.when(d > 0)
    def _():
        for copy in to_dn:
            copy.start()

    def drain(sem, rows):
        view = w2.at[0, pl.ds(0, rows)]
        pltpu.make_async_copy(view, view, sem).wait()

    if not EARLYW:
        build_mixers()
    if not EARLYR:
        build_resample()
    if not EARLYB:
        build_bands()

    row16 = lax.broadcasted_iota(jnp.int32, (16, RC), 0)
    is0, is1, is14, is15 = (row16 == n for n in (0, 1, 14, 15))
    row64 = lax.broadcasted_iota(jnp.int32, (NW, RC), 0)

    def build_s1(e, carry):
        x = g2x[e].astype(F32)
        ahead = pltpu.roll(x, NW - 1, 0)
        behind = pltpu.roll(x, 1, 0)
        s1[e, :, 0:RC] = jnp.where(row64 == NW - 1, 0.0, ahead).astype(BF16)
        s1[e, :, RC : 2 * RC] = g2x[e]
        s1[e, :, 2 * RC :] = jnp.where(row64 == 0, 0.0, behind).astype(BF16)
        t1[e, :, 0:RC] = jnp.where(is1, behind[0:16], 0.0).astype(BF16)
        t1[e, :, 2 * RC :] = jnp.where(is14, ahead[48:64], 0.0).astype(BF16)
        return carry

    def joined(rows, w):
        total = 0.0
        for td in range(3):
            total = total + jnp.dot(
                rows[td], w[3 * td : 3 * td + 3].reshape(3 * RC, RC), preferred_element_type=F32
            )
        return total

    def gated(f, h):
        x = jnp.where(pfx[f].astype(F32) > 0, h, 0.0)
        s2[f, :, 0:RC] = pltpu.roll(x, NW - 1, 0).astype(BF16)
        s2[f, :, RC : 2 * RC] = x.astype(BF16)
        s2[f, :, 2 * RC :] = pltpu.roll(x, 1, 0).astype(BF16)

    def conv1(chunk, carry):
        base = 2 + chunk * CH1
        rows = [s1[pl.ds(base + 2 - td, CH1)].reshape(CH1 * NW, 3 * RC) for td in range(3)]
        total = joined(rows, w2).reshape(CH1, NW, RC)
        for n in range(CH1):
            hidden[base + n, 0:16] = total[n, 0:16]
            hidden[base + n, 16:32] = total[n, 48:64]
            gated(base + n, total[n])
        return carry

    lax.fori_loop(2, 18, build_s1, 0, unroll=2)
    lax.fori_loop(0, 14 // CH1, conv1, 0)

    ld_exp.wait()
    drain(fr_sem.at[0], 96)

    @pl.when(d < ND - 1)
    def _():
        drain(fr_sem.at[2], 224)

    @pl.when(d > 0)
    def _():
        drain(fr_sem.at[1], 224)

    edges[...] = jnp.dot(expm[...], hc[...], preferred_element_type=F32)
    for e in (0, 1, 18, 19):
        build_s1(e, 0)

    def add_edges(e, carry):
        tile = [edges[pl.ds(pl.multiple_of((20 * n + e) * 16, 16), 16)].astype(BF16) for n in range(3)]
        t1[e, :, 0:RC] = t1[e, :, 0:RC] + tile[0]
        t1[e, :, RC : 2 * RC] = tile[1]
        t1[e, :, 2 * RC :] = t1[e, :, 2 * RC :] + tile[2]
        return carry

    lax.fori_loop(0, 20, add_edges, 0, unroll=4)
    fix[...] = joined(
        [t1[2 - td : 20 - td].reshape(18 * 16, 3 * RC) for td in range(3)], w2
    ).reshape(18, 16, RC)
    for f in (0, 16):
        total = joined(
            [s1[f + 2 - td : f + 4 - td].reshape(2 * NW, 3 * RC) for td in range(3)], w2
        ).reshape(2, NW, RC)
        for n in range(2):
            hidden[f + n, 0:16] = total[n, 0:16]
            hidden[f + n, 16:32] = total[n, 48:64]
            gated(f + n, total[n])

    def build_s2(f, carry):
        c = fix[f]
        left = jnp.where(is0, hidden[f, 0:16] + c, hidden[f, 0:16])
        right = jnp.where(is15, hidden[f, 16:32] + c, hidden[f, 16:32])
        left = jnp.where(pfx[f, 0:16].astype(F32) > 0, left, 0.0)
        right = jnp.where(pfx[f, 48:64].astype(F32) > 0, right, 0.0)
        gate = edges[pl.ds(pl.multiple_of((60 + f) * 16, 16), 16)]
        side = jnp.where(gate > 0, c, 0.0)
        s2[f, 0:16, RC : 2 * RC] = left.astype(BF16)
        s2[f, 48:64, RC : 2 * RC] = right.astype(BF16)
        s2[f, 48:64, 0:RC] = jnp.where(is15, pltpu.roll(side, 1, 0), pltpu.roll(right, 15, 0)).astype(BF16)
        s2[f, 0:16, 2 * RC :] = jnp.where(is0, pltpu.roll(side, 15, 0), pltpu.roll(left, 1, 0)).astype(BF16)
        return carry

    lax.fori_loop(0, 18, build_s2, 0, unroll=US2)

    def conv2(chunk, carry):
        base = chunk * CH2
        rows = [s2[pl.ds(base + 2 - td, CH2)].reshape(CH2 * NW, 3 * RC) for td in range(3)]
        total = joined(rows, w1)
        vol[pl.ds(base, CH2)] = total.astype(BF16).reshape(CH2, NW, RC)
        return carry

    lax.fori_loop(0, NS // CH2, conv2, 0, unroll=True)

    def mix(s, carry):
        v = jnp.concatenate([vol[s, :, 0:128], vol[s, :, 128:256]], axis=0)
        y = jnp.dot(v, rt[s], preferred_element_type=F32).astype(BF16)
        for k in range(CAMS):
            ymix[k, s, :, 0:128] = y[0:64, k * 128 : k * 128 + 128]
            ymix[k, s, :, 128:256] = y[64:128, k * 128 : k * 128 + 128]
        return carry

    lax.fori_loop(0, NS, mix, 0, unroll=True)

    block = lax.broadcasted_iota(jnp.int32, (1, 16, 128), 2) // 16

    def back(j, src_row, rows, dst_row, col):
        pltpu.make_async_remote_copy(
            src_ref=zbuf.at[j, pl.ds(src_row, rows)],
            dst_ref=rbuf.at[pl.ds(j * 128 + dst_row, rows)],
            send_sem=bs_sem, recv_sem=br_sem,
            device_id={"depth": lax.rem(d + j, ND), "azim": col},
            device_id_type=pl.DeviceIdType.MESH,
        ).start()

    order = list(range(1, ND)) + [0]
    slots = [
        lax.rem(block - lax.rem(d + j, ND) + ND, ND).astype(F32).astype(BF16) for j in range(ND)
    ]
    for part in range(2):
        source = []
        for k in range(CAMS):
            cam = jnp.dot(
                band[k, part * 64 : part * 64 + 64], ymix[k].reshape(NS * NW, RC),
                preferred_element_type=F32,
            )
            source.append(cam[:, 0:128].astype(BF16).reshape(4, 16, 128))
            source.append(pltpu.roll(cam[:, 128:256], 16, 1).astype(BF16).reshape(4, 16, 128))
        for j in order:
            z = source[0]
            for q in range(1, ROWS):
                z = jnp.where(slots[j] == jnp.asarray(q, BF16), source[q], z)
            if part == 1 and j == 0:
                rbuf[0:64] = z.reshape(64, 128)
                continue
            zbuf[j, part * 64 : part * 64 + 64] = z.reshape(64, 128)
            if part == 0:
                back(j, 0, 32, 64, a_up)
                back(j, 32, 32, 96, a_dn)
            else:
                back(j, 64, 64, 0, a)

    arrived = rbuf.at[pl.ds(64, ND * 128 - 64)]
    pltpu.make_async_copy(arrived, arrived, br_sem).wait()
    total = jnp.zeros((NW, 128), F32)
    for j in range(ND):
        own = rbuf[j * 128 : j * 128 + 64].astype(F32)
        total = total + (own + rbuf[j * 128 + 64 : j * 128 + 128].astype(F32))
    out_ref[0] = pltpu.roll(total, lax.rem(ND - d, ND) * 16, 1)

    pltpu.make_async_copy(arrived, arrived, bs_sem).wait()
    drain(fs_sem.at[0], 96)

    @pl.when(d < ND - 1)
    def _():
        drain(fs_sem.at[1], 224)

    @pl.when(d > 0)
    def _():
        drain(fs_sem.at[2], 224)


def body(cotangent, pre_second, pre_first, kernel_first, kernel_second, row_resample, col_taps, band_width, col_offset):
    consts = [
        jnp.asarray(x, BF16)
        for x in (stage_select(), edge_expand(), row_place(), lane_rows(), sphere_lanes())
    ]
    vm = pltpu.VMEM
    scratch = [
        vm((NS, NW, RC), BF16), vm((NS, NW, RC), BF16), vm((18, NW, RC), BF16),
        vm((20, NW, RC), BF16), vm((2, 9, 96, C), BF16), vm((CAMS, ROWS * ROWS, NS), F32),
        vm((CAMS, TAPS, NS), F32), vm((CAMS, NS), jnp.int32), vm((CAMS, NS), jnp.int32),
        vm((160, 1024), BF16), vm((78 * 16, 160), BF16), vm((2, ROWS, 96, RC), BF16),
        vm((CAMS, ROWS * ROWS, 128), BF16), vm((NS, NS * NW), BF16),
        vm((160, RC), BF16), vm((160, RC), BF16),
        vm((20, NW, 3 * RC), BF16), vm((20, 16, 3 * RC), BF16), vm((18, NW, 3 * RC), BF16),
        vm((18, 32, RC), F32), vm((18, 16, RC), F32), vm((78 * 16, RC), F32), vm((2, 288, 96), BF16),
        vm((9, RC, RC), BF16), vm((9, RC, RC), BF16),
        vm((CAMS * NS * ROWS, 128), F32), vm((NS, 128, CAMS * 128), BF16),
        vm((CAMS, 128, NS * NW), BF16), vm((NS, NW, RC), BF16), vm((CAMS, NS, NW, RC), BF16),
        vm((ROWS, 128, 128), BF16), vm((ND * 128, 128), BF16),
        pltpu.SemaphoreType.DMA((14,)), pltpu.SemaphoreType.DMA((3,)),
        pltpu.SemaphoreType.DMA((3,)), pltpu.SemaphoreType.DMA, pltpu.SemaphoreType.DMA,
    ]
    return pl.pallas_call(
        kernel,
        out_shape=jax.ShapeDtypeStruct((1, NW, 128), F32),
        in_specs=[pl.BlockSpec(memory_space=pl.ANY)] * 14,
        out_specs=pl.BlockSpec(memory_space=pltpu.VMEM),
        scratch_shapes=scratch,
        compiler_params=pltpu.CompilerParams(
            collective_id=0, has_side_effects=True, vmem_limit_bytes=62 * 1024 * 1024
        ),
    )(
        cotangent, pre_second, pre_first,
        kernel_first.reshape(9, 96, C), kernel_second.reshape(9, 96, C),
        row_resample.transpose(0, 2, 3, 1).reshape(CAMS, ROWS * ROWS, NS), col_taps.transpose(0, 2, 1),
        band_width, col_offset, *consts,
    )


def solution(mesh):
    placed = (
        P("depth", "azim", None),
        P("depth", "azim", None),
        P("depth", "azim", None),
        P(),
        P(),
        P(None, "depth", None, None),
        P(None, "depth", None),
        P(None, "depth"),
        P(None, "depth"),
    )
    return jax.shard_map(
        body, mesh=mesh, in_specs=placed, out_specs=P("depth", "azim", None), check_vma=False
    )
```

time: 32.1 us -> 30.9 us (0.963)
  Pallas kernels: 30.4 us -> 29.3 us
    pallas_call x1, Pallas kernels: 30.4 us -> 29.3 us  [body(): pl.pallas_call(kernel, out_shape=jax.ShapeDtypeStruct((1, NW, 128), F32),...]
where the time goes in v3:
time: 30.9 us; the launch traced here: 30.7 us
  Pallas kernels  29.3 us (95%)
  local copies, waits for them, and re-layouts  1.38 us (4%)
    pallas_call x1, Pallas kernels, body(): pl.pallas_call(kernel, out_shape=jax.ShapeDtypeStruct((1, NW, 128), F32),...  29.3 us
    unnamed x1, local copies, waits for them, and re-layouts  1.38 us

profile of v3, /device:TPU:1, one launch (start us, length us, event | category | flops | bytes accessed | tf_op | source)
XLA Modules:
  0.0 30.7 jit_solution(4857201855390443756)
XLA Ops:
  0.0 29.3 %shard_map.136 = f32[1,64,128]{2,1,0:T(8,128)} custom-call(bf16[16,64,256]{2,1,0:T(8,128)(2,1)} %cot_h.1, bf16[16,64,256]{2,1,0:T(8,128)(2,1)} %pre2_h.1, bf16[16,64,256]{2,1,0:T(8,128)(2,1)} %pre1_h.1, bf16[9,96,32]{2,1,0:T(8,128)(2,1)} %bitcast.6, bf16[9,96,32]{2,1,0:T(8,128)(2,1)} %bitcast.7, f32[4,64,16]{2,1,0:T(8,128)} %bitcast.8, f32[4,8,16]{2,1,0:T(8,128)} %bitcast.9, ...), custom_call_target="tpu_custom_call" | custom-call | tf_op jit(solution)/shard_map/pallas_call | solution.py:501
  29.3 1.4 %copy.16 = f32[1,64,128]{2,1,0:T(8,128)} copy(f32[1,64,128]{2,1,0:T(8,128)} %shard_map.136) | data formatting | bytes 65536

commit v4 on v3

--- a/solution.py
+++ b/solution.py
@@ -17,9 +17,7 @@
 ND = 8
 F32 = jnp.float32
 BF16 = jnp.bfloat16
-EARLYB = 1
-EARLYR = 0
-EARLYW = 0
+PARTS = 1
 US2 = 3
 CH1 = 7
 CH2 = 8
@@ -93,18 +91,12 @@
     return out.reshape(CAMS, ROWS * ROWS, 128)
 
 
-def sphere_lanes():
-    out = np.zeros((NS, NS * NW), np.float32)
-    out[np.arange(NS * NW) // NW, np.arange(NS * NW)] = 1
-    return out
-
-
 def kernel(
     cot_h, pre2_h, pre1_h, k1_h, k2_h, rr_h, taps_h, width_h, off_h,
-    sel_h, exp_h, place_h, lrow_h, slane_h,
+    sel_h, exp_h, place_h, lrow_h,
     out_ref,
     cot, pre2, pfx, g2x, kk, rr, taps, width, off,
-    sel, expm, place, lrow, slane,
+    sel, expm, place, lrow, base,
     stage, hc, s1, t1, s2, hidden, fix, edges, kc, w2, w1, lbuf, rt, band, vol, ymix, zbuf, rbuf,
     in_sem, fs_sem, fr_sem, bs_sem, br_sem,
 ):
@@ -119,14 +111,14 @@
         copy.start()
         return copy
 
-    ld_cot = load(0, cot_h, cot)
-    ld_pre2 = load(1, pre2_h, pre2)
+    ld_parts = []
+    for part in range(PARTS):
+        span = pl.ds(part * (NS // PARTS), NS // PARTS)
+        ld_parts.append(load(13 + 2 * part, cot_h.at[span], cot.at[span]))
+        ld_parts.append(load(14 + 2 * part, pre2_h.at[span], pre2.at[span]))
     ld_taps = load(9, taps_h, taps)
     ld_width = load(10, width_h, width)
     ld_off = load(11, off_h, off)
-    ld_slane = load(12, slane_h, slane)
-    ld_pre1 = load(2, pre1_h, pfx.at[pl.ds(1, NS)])
-    ld_sel = load(3, sel_h, sel)
 
     barrier = pltpu.get_barrier_semaphore()
     for j in range(ND):
@@ -139,12 +131,14 @@
                 device_id_type=pl.DeviceIdType.MESH,
             )
 
+    ld_pre1 = load(2, pre1_h, pfx.at[pl.ds(1, NS)])
+    ld_sel = load(3, sel_h, sel)
     ld_rr = load(7, rr_h, rr)
     ld_lrow = load(8, lrow_h, lrow)
     ld_k2 = load(4, k2_h, kk.at[0])
     ld_place = load(6, place_h, place)
     ld_k1 = load(5, k1_h, kk.at[1])
-    ld_exp = load(13, exp_h, expm)
+    ld_exp = load(1, exp_h, expm)
 
     @pl.when(d == 0)
     def _():
@@ -157,6 +151,10 @@
         g2x[18:20] = jnp.zeros((2, NW, RC), BF16)
         pfx[17:18] = jnp.zeros((1, NW, RC), BF16)
         hc[128:160] = jnp.zeros((32, RC), BF16)
+
+    eye16 = (
+        lax.broadcasted_iota(jnp.int32, (NS, NS), 0) == lax.broadcasted_iota(jnp.int32, (NS, NS), 1)
+    ).astype(BF16)
 
     def build_mixers():
         ld_k2.wait()
@@ -177,9 +175,6 @@
     def build_resample():
         ld_rr.wait()
         ld_lrow.wait()
-        eye16 = (
-            lax.broadcasted_iota(jnp.int32, (NS, NS), 0) == lax.broadcasted_iota(jnp.int32, (NS, NS), 1)
-        ).astype(BF16)
         own_row = (
             lax.broadcasted_iota(jnp.int32, (ROWS * NS, ROWS * ROWS), 0) // NS
             == lax.broadcasted_iota(jnp.int32, (ROWS * NS, ROWS * ROWS), 1) // ROWS
@@ -211,40 +206,52 @@
         ld_taps.wait()
         ld_width.wait()
         ld_off.wait()
-        ld_slane.wait()
-        lanes = NS * NW
-        width_l = jnp.dot(width[...].astype(F32).astype(BF16), slane[...], preferred_element_type=F32)
-        off_l = jnp.dot(off[...].astype(F32).astype(BF16), slane[...], preferred_element_type=F32)
-        tap_index = lax.broadcasted_iota(jnp.int32, (TAPS, lanes), 0).astype(F32)
-        u_lane = lax.rem(lax.broadcasted_iota(jnp.int32, (1, lanes), 1), NW).astype(F32)
-        w_row = lax.broadcasted_iota(jnp.int32, (16, lanes), 0).astype(F32).astype(BF16)
+        def turned(x):
+            return lax.dot_general(
+                eye16, x.astype(F32).astype(BF16), (((1,), (1,)), ((), ())),
+                preferred_element_type=F32,
+            )
+
+        offs, widths = turned(off[...]), turned(width[...])
+        lane = lax.broadcasted_iota(jnp.int32, (NS, 128), 1)
+        odd = lax.rem(lax.broadcasted_iota(jnp.int32, (NS, 128), 0), 2)
+        place_lane = lax.rem(lane - 64 * odd + 128, 128).astype(F32)
+        low = lax.broadcasted_iota(jnp.int32, (128, 128), 1) < 64
         for k in range(CAMS):
-            taps_l = jnp.dot(taps[k].astype(BF16), slane[...], preferred_element_type=F32)
-            taps_l = jnp.where(tap_index < width_l[k : k + 1], taps_l, 0.0)
-            wide = [
-                jnp.broadcast_to(taps_l[j : j + 1], (16, lanes)).astype(BF16) for j in range(TAPS)
-            ]
-            start = jnp.broadcast_to(u_lane + 32.0 - off_l[k : k + 1], (16, lanes)).astype(BF16) - w_row
-
-            def build_band(block, carry):
-                gap = start - lax.rem(block * 16 + 96, 128).astype(F32).astype(BF16)
-                value = jnp.zeros((16, lanes), BF16)
-                for j in range(TAPS):
-                    value = jnp.where(gap == jnp.asarray(j, BF16), wide[j], value)
-                band[k, pl.ds(pl.multiple_of(block * 16, 16), 16)] = value
-                return carry
-
-            lax.fori_loop(0, 8, build_band, 0)
-
-    if EARLYB:
-        build_bands()
-    if EARLYR:
-        build_resample()
-    if EARLYW:
-        build_mixers()
-    ld_cot.wait()
-    ld_pre2.wait()
-    g2x[2:18] = jnp.where(pre2[...] > 0, cot[...], jnp.zeros((), BF16))
+            tap = turned(taps[k])
+            start = offs[:, k : k + 1] - 32.0
+            start = jnp.where(start < 0, start + 128.0, start)
+            gap = place_lane - start
+            gap = jnp.where(gap < 0, gap + 128.0, gap)
+            value = jnp.zeros((NS, 128), F32)
+            for j in range(TAPS):
+                keep = (gap == float(j)) & (widths[:, k : k + 1] > float(j))
+                value = jnp.where(keep, tap[:, j : j + 1], value)
+            base[k] = value
+        def roll_bands(pair, carry):
+            for k in range(CAMS):
+                two = [
+                    pltpu.roll(
+                        jnp.broadcast_to(base[k, pl.ds(2 * pair + n, 1)], (128, 128)),
+                        96, 1, stride=1, stride_axis=0,
+                    )
+                    for n in range(2)
+                ]
+                band[k, :, pl.ds(pl.multiple_of(pair * 128, 128), 128)] = jnp.where(
+                    low, two[0], two[1]
+                ).astype(BF16)
+            return carry
+
+        lax.fori_loop(0, NS // 2, roll_bands, 0)
+
+    build_bands()
+    for part in range(PARTS):
+        ld_parts[2 * part].wait()
+        ld_parts[2 * part + 1].wait()
+        span = pl.ds(part * (NS // PARTS), NS // PARTS)
+        g2x[pl.ds(2 + part * (NS // PARTS), NS // PARTS)] = jnp.where(
+            pre2[span] > 0, cot[span], jnp.zeros((), BF16)
+        )
     ld_pre1.wait()
     ld_sel.wait()
     acc = jnp.zeros((160, RC), F32)
@@ -299,12 +306,8 @@
         view = w2.at[0, pl.ds(0, rows)]
         pltpu.make_async_copy(view, view, sem).wait()
 
-    if not EARLYW:
-        build_mixers()
-    if not EARLYR:
-        build_resample()
-    if not EARLYB:
-        build_bands()
+    build_mixers()
+    build_resample()
 
     row16 = lax.broadcasted_iota(jnp.int32, (16, RC), 0)
     is0, is1, is14, is15 = (row16 == n for n in (0, 1, 14, 15))
@@ -479,7 +482,7 @@
 def body(cotangent, pre_second, pre_first, kernel_first, kernel_second, row_resample, col_taps, band_width, col_offset):
     consts = [
         jnp.asarray(x, BF16)
-        for x in (stage_select(), edge_expand(), row_place(), lane_rows(), sphere_lanes())
+        for x in (stage_select(), edge_expand(), row_place(), lane_rows())
     ]
     vm = pltpu.VMEM
     scratch = [
@@ -487,7 +490,7 @@
         vm((20, NW, RC), BF16), vm((2, 9, 96, C), BF16), vm((CAMS, ROWS * ROWS, NS), F32),
         vm((CAMS, TAPS, NS), F32), vm((CAMS, NS), jnp.int32), vm((CAMS, NS), jnp.int32),
         vm((160, 1024), BF16), vm((78 * 16, 160), BF16), vm((2, ROWS, 96, RC), BF16),
-        vm((CAMS, ROWS * ROWS, 128), BF16), vm((NS, NS * NW), BF16),
+        vm((CAMS, ROWS * ROWS, 128), BF16), vm((CAMS, NS, 128), F32),
         vm((160, RC), BF16), vm((160, RC), BF16),
         vm((20, NW, 3 * RC), BF16), vm((20, 16, 3 * RC), BF16), vm((18, NW, 3 * RC), BF16),
         vm((18, 32, RC), F32), vm((18, 16, RC), F32), vm((78 * 16, RC), F32), vm((2, 288, 96), BF16),
@@ -495,13 +498,13 @@
         vm((CAMS * NS * ROWS, 128), F32), vm((NS, 128, CAMS * 128), BF16),
         vm((CAMS, 128, NS * NW), BF16), vm((NS, NW, RC), BF16), vm((CAMS, NS, NW, RC), BF16),
         vm((ROWS, 128, 128), BF16), vm((ND * 128, 128), BF16),
-        pltpu.SemaphoreType.DMA((14,)), pltpu.SemaphoreType.DMA((3,)),
+        pltpu.SemaphoreType.DMA((13 + 2 * PARTS,)), pltpu.SemaphoreType.DMA((3,)),
         pltpu.SemaphoreType.DMA((3,)), pltpu.SemaphoreType.DMA, pltpu.SemaphoreType.DMA,
     ]
     return pl.pallas_call(
         kernel,
         out_shape=jax.ShapeDtypeStruct((1, NW, 128), F32),
-        in_specs=[pl.BlockSpec(memory_space=pl.ANY)] * 14,
+        in_specs=[pl.BlockSpec(memory_space=pl.ANY)] * 13,
         out_specs=pl.BlockSpec(memory_space=pltpu.VMEM),
         scratch_shapes=scratch,
         compiler_params=pltpu.CompilerParams(

time: 30.9 us -> 31 us (level)
  no operation moved by 1% of the time
where the time goes in v4:
time: 31 us; the launch traced here: 30.8 us
  Pallas kernels  29.4 us (95%)
  local copies, waits for them, and re-layouts  1.38 us (4%)
    pallas_call x1, Pallas kernels, body(): pl.pallas_call(kernel, out_shape=jax.ShapeDtypeStruct((1, NW, 128), F32),...  29.4 us
    unnamed x1, local copies, waits for them, and re-layouts  1.38 us

profile of v4, /device:TPU:1, one launch (start us, length us, event | category | flops | bytes accessed | tf_op | source)
XLA Modules:
  0.0 30.8 jit_solution(15929682355476252713)
XLA Ops:
  0.0 29.4 %shard_map.127 = f32[1,64,128]{2,1,0:T(8,128)} custom-call(bf16[16,64,256]{2,1,0:T(8,128)(2,1)} %cot_h.1, bf16[16,64,256]{2,1,0:T(8,128)(2,1)} %pre2_h.1, bf16[16,64,256]{2,1,0:T(8,128)(2,1)} %pre1_h.1, bf16[9,96,32]{2,1,0:T(8,128)(2,1)} %bitcast.6, bf16[9,96,32]{2,1,0:T(8,128)(2,1)} %bitcast.7, f32[4,64,16]{2,1,0:T(8,128)} %bitcast.8, f32[4,8,16]{2,1,0:T(8,128)} %bitcast.9, ...), custom_call_target="tpu_custom_call" | custom-call | tf_op jit(solution)/shard_map/pallas_call | solution.py:504
  29.4 1.4 %copy.15 = f32[1,64,128]{2,1,0:T(8,128)} copy(f32[1,64,128]{2,1,0:T(8,128)} %shard_map.127) | data formatting | bytes 65536

commit v5 on v4

--- a/solution.py
+++ b/solution.py
@@ -124,7 +124,7 @@
     for j in range(ND):
         t = lax.rem(d + j, ND)
         for col in (a_dn, a, a_up):
-            if j == 0 and col is a:
+            if (j == 0 and col is a) or (1 < j < ND - 1 and col is not a):
                 continue
             pl.semaphore_signal(
                 barrier, inc=1, device_id={"depth": t, "azim": col},
@@ -263,7 +263,7 @@
         )
     stage[...] = acc.astype(BF16)
 
-    pl.semaphore_wait(barrier, 3 * ND - 1)
+    pl.semaphore_wait(barrier, ND + 5)
 
     def remote(group, src, dst, dep, col):
         return pltpu.make_async_remote_copy(

time: 31 us -> 30.5 us (0.984); the launches traced: 30.8 us -> 29.9 us
  Pallas kernels: 29.4 us -> 28.5 us
    pallas_call x1, Pallas kernels: 29.4 us -> 28.5 us  [body(): pl.pallas_call(kernel, out_shape=jax.ShapeDtypeStruct((1, NW, 128), F32),...]
where the time goes in v5:
time: 30.5 us; the launch traced here: 29.9 us
  Pallas kernels  28.5 us (93%)
  local copies, waits for them, and re-layouts  1.38 us (5%)
    pallas_call x1, Pallas kernels, body(): pl.pallas_call(kernel, out_shape=jax.ShapeDtypeStruct((1, NW, 128), F32),...  28.5 us
    unnamed x1, local copies, waits for them, and re-layouts  1.38 us

profile of v5, /device:TPU:1, one launch (start us, length us, event | category | flops | bytes accessed | tf_op | source)
XLA Modules:
  0.0 29.9 jit_solution(11831129691791424090)
XLA Ops:
  0.0 28.5 %shard_map.127 = f32[1,64,128]{2,1,0:T(8,128)} custom-call(bf16[16,64,256]{2,1,0:T(8,128)(2,1)} %cot_h.1, bf16[16,64,256]{2,1,0:T(8,128)(2,1)} %pre2_h.1, bf16[16,64,256]{2,1,0:T(8,128)(2,1)} %pre1_h.1, bf16[9,96,32]{2,1,0:T(8,128)(2,1)} %bitcast.6, bf16[9,96,32]{2,1,0:T(8,128)(2,1)} %bitcast.7, f32[4,64,16]{2,1,0:T(8,128)} %bitcast.8, f32[4,8,16]{2,1,0:T(8,128)} %bitcast.9, ...), custom_call_target="tpu_custom_call" | custom-call | tf_op jit(solution)/shard_map/pallas_call | solution.py:504
  28.5 1.4 %copy.15 = f32[1,64,128]{2,1,0:T(8,128)} copy(f32[1,64,128]{2,1,0:T(8,128)} %shard_map.127) | data formatting | bytes 65536
